TPU v7x, 512 devices: a whole 4x8x8 slice. The times are simulated.
512 devices in a mesh: row: 16 (over y, core), col: 32 (over x, z).
Axes of the slice: x: 4, y: 8, z: 8, core: 2. Of those that a mesh axis runs over, the one named last changes fastest.
Arguments:
- hidden_acts: bfloat16 [256, 29568], P('row', 'col'), may hold values from -6 to 6
- output_errors: bfloat16 [256, 4096], P('col', 'row'), may hold values from -6 to 6
- col_points: int32 [32], replicated, may hold values from 0 to 64, as said below
- row_points: int32 [16], replicated, may hold values from 0 to 32, as said below
- worker_mask: int32 [16, 32], replicated, may hold values from 0 to 1, as said below
Outputs:
- clipped_grad: float32 [8, 512, 29568], P(None, 'col', 'row')
Inputs may be any that keep to these rules, and one draw needn't show every extreme that they name: `col_points`: distinct node indices. `row_points`: distinct node indices. `worker_mask`: each row of the grid has between 1 and 8 erased workers.
All inputs are finite; a program needn't handle non-finite values.
Results may differ from a plain program's by a relative error of at most 0.02.
Values may be sent and summed in bfloat16 or wider, within the bound.
No kernel may reach another device: no remote copies, remote signals or barrier semaphores. Data moves between devices by JAX's collectives and lax.ppermute only.
A program may use at most 128 MiB of HBM per device.

v0:
```python
import jax
import jax.numpy as jnp
from jax import lax
from jax.sharding import Mesh
from jax.sharding import PartitionSpec as P

D = 4096
FF = 29568
COL = ("col_0", "col_1")
ROW = ("row_0", "row_1")
ROW_COL = ("row_0", "row_1", "col_0", "col_1")


def copy_for_each(shard, axis):
    peers = lax.axis_size(axis)
    return lax.all_to_all(
        jnp.broadcast_to(shard[None], (peers, *shard.shape)), axis, 0, 0, tiled=True
    )


def laid_out(blocks, dim):
    lengths = list(blocks.shape[1:])
    lengths[dim] *= blocks.shape[0]
    return jnp.moveaxis(blocks, 0, dim).reshape(lengths)


def gathered_copies(shard, axis, dim):
    blocks = copy_for_each(shard, axis)
    return laid_out(blocks, dim)


def one_axis_at_a_time(shard, axes):
    for axis in axes:
        shard = lax.psum(shard, axis)
    return shard


def node_value(index, count):
    return jnp.cos(jnp.pi * (2.0 * index.astype(jnp.float32) + 1.0) / (2.0 * count))


def berrut(nodes, signs, live, targets):
    terms = (live * signs)[:, None] / (targets[None, :] - nodes[:, None])
    return terms / jnp.sum(terms, axis=0, keepdims=True)


def rank_signs(points, live):
    lower = (points[None, :] < points[:, None]).astype(jnp.int32)
    ranks = jnp.sum(lower * live[None, :], axis=1)
    return (1 - 2 * (ranks % 2)).astype(jnp.float32)


def encode_blocks(source, weights, block_count, block_width):

    def add_block(index, total):
        piece = lax.dynamic_slice_in_dim(source, index * block_width, block_width, 1).astype(
            jnp.float32
        )
        factor = lax.dynamic_slice_in_dim(weights, index, 1, 0)
        return total + factor * piece

    start = jnp.zeros((source.shape[0], block_width), jnp.float32)
    return lax.fori_loop(0, block_count, add_block, start).astype(jnp.bfloat16)


def shards(hidden_acts, output_errors, col_points, row_points, worker_mask):
    col_count = lax.axis_size(COL)
    row_count = lax.axis_size(ROW)
    col_place = lax.axis_index(COL)
    row_place = lax.axis_index(ROW)
    act_blocks = col_count // 2
    err_blocks = row_count // 2
    act_width = FF // act_blocks
    err_width = D // err_blocks
    data_acts = node_value(jnp.arange(act_blocks), act_blocks)
    data_errs = node_value(jnp.arange(err_blocks), err_blocks)
    work_acts = node_value(col_points, 2 * col_count + 1)
    work_errs = node_value(row_points, 2 * row_count + 1)
    alt_acts = (1 - 2 * (jnp.arange(act_blocks) % 2)).astype(jnp.float32)
    alt_errs = (1 - 2 * (jnp.arange(err_blocks) % 2)).astype(jnp.float32)
    full_acts = gathered_copies(hidden_acts, COL, 1)
    own_node = lax.dynamic_slice_in_dim(work_acts, col_place, 1, 0)
    encode_own = berrut(data_acts, alt_acts, jnp.ones((act_blocks,), jnp.float32), own_node)[:, 0]
    coded_acts = encode_blocks(full_acts, encode_own, act_blocks, act_width)
    full_errs = lax.all_gather(output_errors, ROW, axis=1, tiled=True)
    own_err = lax.dynamic_slice_in_dim(work_errs, row_place, 1, 0)
    encode_err = berrut(data_errs, alt_errs, jnp.ones((err_blocks,), jnp.float32), own_err)[:, 0]
    coded_errs = encode_blocks(full_errs, encode_err, err_blocks, err_width)
    all_errs = gathered_copies(coded_errs, COL, 0)
    product = lax.dot_general(
        all_errs,
        lax.all_gather(coded_acts, ROW, axis=0, tiled=True),
        (((0,), (0,)), ((), ())),
        preferred_element_type=jnp.float32,
    ).astype(jnp.bfloat16)
    live = lax.dynamic_slice_in_dim(worker_mask, row_place, 1, 0)[0]
    decode_acts = berrut(
        work_acts, rank_signs(col_points, live), live.astype(jnp.float32), data_acts
    )
    decoded = jnp.einsum(
        "jk,jrf->rkf",
        decode_acts,
        lax.all_to_all(product[None], COL, split_axis=1, concat_axis=0, tiled=True).astype(
            jnp.float32
        ),
    ).astype(jnp.bfloat16)
    decoded = decoded.reshape(decoded.shape[0], FF)
    all_rows = jnp.ones((row_count,), jnp.int32)
    decode_errs = berrut(
        work_errs, rank_signs(row_points, all_rows), jnp.ones((row_count,), jnp.float32), data_errs
    )
    grad = jnp.einsum(
        "il,irf->lrf",
        decode_errs,
        lax.all_to_all(decoded[None], ROW, split_axis=2, concat_axis=0, tiled=True).astype(
            jnp.float32
        ),
    )
    squares = one_axis_at_a_time(jnp.sum(grad * grad), ROW_COL)
    factor = jnp.minimum(1.0, jnp.sqrt(jnp.float32(FF * D)) / jnp.sqrt(squares + 1e-06))
    return grad * factor


def solution(mesh):
    finer = Mesh(mesh.devices.reshape(8, 2, 4, 8), ("row_0", "row_1", "col_0", "col_1"))
    in_specs = (P(ROW, COL), P(COL, ROW), P(), P(), P())
    out_specs = P(None, COL, ROW)
    return jax.shard_map(
        shards, mesh=finer, in_specs=in_specs, out_specs=out_specs, check_vma=False
    )
```

profile of v0, /device:TPU:1, one launch (start us, length us, event | category | flops | bytes accessed | tf_op | source)
XLA Modules:
  0.0 505.8 jit_solution(16859528297942924830)
XLA Ops:
  0.0 1.9 broadcast_in_dim.19
  1.9 13.7 %all-to-all-start.1 = ((bf16[32,16,924]{2,1,0:T(8,128)(2,1)}), bf16[32,16,924]{2,1,0:T(8,128)(2,1)S(1)}, u32[]{:S(2)}, u32[]{:S(2)}) async-start(bf16[32,16,924]{2,1,0:T(8,128)(2,1)} %broadcast_in_dim.19), calls=%async_computation.1 | async-start | bytes 2097152 | tf_op jit(solution)/shard_map/all_to_all | solution.py:16
  16.3 1.2 divide_reduce_fusion.1
  17.6 1.2 multiply_divide_fusion.1
  18.8 18.5 %all_gather.6 = bf16[8,4096]{1,0:T(8,128)(2,1)S(1)} all-gather(bf16[8,256]{1,0:T(8,128)(2,1)S(1)} %copy-done.1), channel_id=1, replica_groups=mesh['row_0'=8,'row_1'=2,'col_0'=4,'col_1'=8] {'row_0','row_1'}, dimensions={1}, use_global_device_ids=true | all-gather | bytes 69632 | tf_op jit(solution)/shard_map/all_gather | solution.py:85
  37.4 9.4 %while.28 = (s32[]{:T(128)}, f32[8,512]{1,0:T(8,128)S(1)}, f32[8]{0:T(128)S(1)}, bf16[8,4096]{1,0:T(8,128)(2,1)S(1)}, s32[]{:T(128)}, /*index=5*/s32[]{:T(128)}, s32[]{:T(128)}, s32[]{:T(128)}) while((s32[]{:T(128)}, f32[8,512]{1,0:T(8,128)S(1)}, f32[8]{0:T(128)S(1)}, bf16[8,4096]{1,0:T(8,128)(2,1)S(1)}, s32[]{:T(128)}, ...), condition=%wide.region_4.5_spmd.clone, body=%wide.region_3.4_spmd.clone.sunk | while | flops 16391 | bytes 41121 | solution.py:63
  49.0 1.3 divide_reduce_fusion
  50.3 1.3 multiply_divide_fusion
  52.3 9.5 %all-to-all-start = ((bf16[32,8,512]{2,1,0:T(8,128)(2,1)}), bf16[32,8,512]{2,1,0:T(8,128)(2,1)S(1)}, u32[]{:S(2)}, u32[]{:S(2)}) async-start(bf16[32,8,512]{2,1,0:T(8,128)(2,1)} %broadcast_in_dim.16), calls=%async_computation | async-start | bytes 524288 | tf_op jit(solution)/shard_map/all_to_all | solution.py:16
  62.4 1.3 reshape.108
  63.6 23.7 %while.29 = (s32[]{:T(128)}, f32[16,1848]{1,0:T(8,128)S(1)}, f32[16]{0:T(128)S(1)}, bf16[16,29568]{1,0:T(8,128)(2,1)S(1)}, s32[]{:T(128)}, /*index=5*/s32[]{:T(128)}, s32[]{:T(128)}, s32[]{:T(128)}) while((s32[]{:T(128)}, f32[16,1848]{1,0:T(8,128)S(1)}, f32[16]{0:T(128)S(1)}, bf16[16,29568]{1,0:T(8,128)(2,1)S(1)}, s32[]{:T(128)}, ...), condition=%wide.region_7.8_spmd.clone, body=%wide.region_6.7_spmd.clone.sunk | while | flops 118279 | bytes 295841 | solution.py:63
  64.3 0.8 select_add_fusion.5
  65.8 0.8 select_add_fusion.5
  67.3 0.8 select_add_fusion.5
  68.8 0.8 select_add_fusion.5
  70.3 0.8 select_add_fusion.5
  71.7 0.8 select_add_fusion.5
  73.2 0.8 select_add_fusion.5
  74.7 0.8 select_add_fusion.5
  76.2 0.8 select_add_fusion.5
  77.7 0.8 select_add_fusion.5
  79.1 0.8 select_add_fusion.5
  82.1 0.8 select_add_fusion.5
  83.6 0.8 select_add_fusion.5
  86.5 0.8 select_add_fusion.5
  87.4 17.9 %all_gather.7 = bf16[256,1848]{1,0:T(8,128)(2,1)S(1)} all-gather(bf16[16,1848]{1,0:T(8,128)(2,1)S(1)} %convert_element_type.115), channel_id=1, replica_groups=mesh['row_0'=8,'row_1'=2,'col_0'=4,'col_1'=8] {'row_0','row_1'}, dimensions={0}, use_global_device_ids=true | all-gather | bytes 1005312 | tf_op jit(solution)/shard_map/all_gather | solution.py:92
  106.0 6.8 %copy.23 = bf16[1,512,1848]{2,0,1:T(2,128)(2,1)} copy(bf16[1,512,1848]{1,2,0:T(8,128)(2,1)S(1)} %fusion) | data formatting | bytes 3784704 | tf_op jit(solution)/shard_map/broadcast_in_dim | solution.py:103
  113.3 12.9 %reduce.2 = bf16[512,1848]{1,0:T(8,128)(2,1)S(1)} reduce(bf16[512,1,1848]{2,1,0:T(2,128)(2,1)} %bitcast.43, bf16[]{:T(256)} %broadcast.315), dimensions={1}, to_apply=%bitcast.26.reduce_sub_computation | reduce | bytes 3784706
  126.2 4.5 reshape.111
  130.7 9.7 %all-to-all-start.2 = ((bf16[32,2,14784]{2,1,0:T(2,128)(2,1)}), bf16[32,2,14784]{2,1,0:T(2,128)(2,1)S(1)}, u32[]{:S(2)}, u32[]{:S(2)}) async-start(bf16[32,2,14784]{2,1,0:T(2,128)(2,1)} %reshape.111), calls=%async_computation.2 | async-start | bytes 3801088 | tf_op jit(solution)/shard_map/all_to_all | solution.py:103
  140.6 44.4 %all-to-all-done.2 = bf16[32,2,14784]{2,1,0:T(2,128)(2,1)S(1)} async-done(((bf16[32,2,14784]{2,1,0:T(2,128)(2,1)}), bf16[32,2,14784]{2,1,0:T(2,128)(2,1)S(1)}, u32[]{:S(2)}, u32[]{:S(2)}) %all-to-all-start.2) | async-done | bytes 1892384 | tf_op jit(solution)/shard_map/all_to_all | solution.py:103
  185.0 7.4 %reshape.112 = bf16[512,1,1848]{2,1,0:T(2,128)(2,1)} reshape(bf16[32,2,14784]{2,1,0:T(2,128)(2,1)S(1)} %all-to-all-done.2) | data formatting | bytes 3784704
  192.4 2.4 copy.28
  195.3 1.0 broadcast_in_dim_reshape.3
  196.3 22.8 %copy.25 = bf16[1,16,29568]{1,0,2:T(2,128)(2,1)} copy(bf16[1,16,29568]{2,1,0:T(8,128)(2,1)S(1)} %broadcast_in_dim_reshape.3) | data formatting | bytes 1892352 | tf_op jit(solution)/shard_map/broadcast_in_dim;reshape | solution.py:115
  219.1 162.1 %reduce.3 = bf16[29568,16]{1,0:T(8,128)(2,1)} reduce(bf16[29568,1,16]{2,1,0:T(2,128)(2,1)} %bitcast.41, bf16[]{:T(256)} %broadcast.315), dimensions={1}, to_apply=%bitcast.28.reduce_sub_computation | reduce | bytes 1892354
  381.2 10.5 %reshape.113 = bf16[16,2,14784]{2,1,0:T(2,128)(2,1)} reshape(bf16[29568,16]{1,0:T(8,128)(2,1)} %reduce.3) | data formatting | bytes 1892352
  391.7 7.0 %all-to-all-start.3 = ((bf16[16,2,14784]{2,1,0:T(2,128)(2,1)}), bf16[16,2,14784]{2,1,0:T(2,128)(2,1)S(1)}, u32[]{:S(2)}, u32[]{:S(2)}) async-start(bf16[16,2,14784]{2,1,0:T(2,128)(2,1)} %reshape.113), calls=%async_computation.3 | async-start | bytes 1900544 | tf_op jit(solution)/shard_map/all_to_all | solution.py:115
  399.1 25.5 %all-to-all-done.3 = bf16[16,2,14784]{2,1,0:T(2,128)(2,1)S(1)} async-done(((bf16[16,2,14784]{2,1,0:T(2,128)(2,1)}), bf16[16,2,14784]{2,1,0:T(2,128)(2,1)S(1)}, u32[]{:S(2)}, u32[]{:S(2)}) %all-to-all-start.3) | async-done | bytes 946208 | tf_op jit(solution)/shard_map/all_to_all | solution.py:115
  424.7 11.2 %reshape.114 = bf16[29568,1,16]{2,1,0:T(2,128)(2,1)} reshape(bf16[16,2,14784]{2,1,0:T(2,128)(2,1)S(1)} %all-to-all-done.3) | data formatting | bytes 1892352
  435.9 27.1 %copy.26 = bf16[1,16,29568]{2,1,0:T(8,128)(2,1)S(1)} copy(bf16[1,16,29568]{1,0,2:T(2,128)(2,1)} %bitcast.42) | data formatting | bytes 1892352 | tf_op jit(solution)/shard_map/all_to_all | solution.py:115
  463.0 1.6 all_to_all.33
  464.6 1.1 multiply_reduce_fusion
  465.6 11.3 %psum.28 = f32[]{:T(128)} all-reduce(f32[]{:T(128)} %get-tuple-element.211), channel_id=1, replica_groups=mesh['row_0'=8,'row_1'=2,'col_0'=4,'col_1'=8] {'row_0'}, use_global_device_ids=true, to_apply=%region_11.12 | all-reduce | flops 1 | bytes 8 | tf_op jit(solution)/shard_map/psum | solution.py:34
  477.0 6.3 %psum.29 = f32[]{:T(128)} all-reduce(f32[]{:T(128)} %psum.28), channel_id=1, replica_groups=mesh['row_0'=8,'row_1'=2,'col_0'=4,'col_1'=8] {'row_1'}, use_global_device_ids=true, to_apply=%region_12.13 | all-reduce | flops 1 | bytes 8 | tf_op jit(solution)/shard_map/psum | solution.py:34
  483.2 7.1 %psum.30 = f32[]{:T(128)} all-reduce(f32[]{:T(128)} %psum.29), channel_id=1, replica_groups=mesh['row_0'=8,'row_1'=2,'col_0'=4,'col_1'=8] {'col_0'}, use_global_device_ids=true, to_apply=%region_13.14 | all-reduce | flops 1 | bytes 8 | tf_op jit(solution)/shard_map/psum | solution.py:34
  490.4 13.5 %psum.31 = f32[]{:T(128)} all-reduce(f32[]{:T(128)} %psum.30), channel_id=1, replica_groups=mesh['row_0'=8,'row_1'=2,'col_0'=4,'col_1'=8] {'col_1'}, use_global_device_ids=true, to_apply=%region_14.15 | all-reduce | flops 1 | bytes 8 | tf_op jit(solution)/shard_map/psum | solution.py:34
  504.7 1.1 copy.27
  (64 shorter events, 28.1 us)
Async XLA Ops:
  0.0 15.7 %copy-start.2 = (s32[16]{0:T(128)S(1)}, s32[16]{0:T(128)}, u32[]{:S(2)}) copy-start(s32[16]{0:T(128)} %param.12) | copy-start | bytes 196
  0.0 18.8 %copy-start.1 = (bf16[8,256]{1,0:T(8,128)(2,1)S(1)}, bf16[8,256]{1,0:T(8,128)(2,1)}, u32[]{:S(2)}) copy-start(bf16[8,256]{1,0:T(8,128)(2,1)} %param.10) | copy-start | bytes 12292
  0.0 47.5 %copy-start = (s32[32]{0:T(128)S(1)}, s32[32]{0:T(128)}, u32[]{:S(2)}) copy-start(s32[32]{0:T(128)} %param.11) | copy-start | bytes 388
  1.9 49.6 %all-to-all-start.1 = ((bf16[32,16,924]{2,1,0:T(8,128)(2,1)}), bf16[32,16,924]{2,1,0:T(8,128)(2,1)S(1)}, u32[]{:S(2)}, u32[]{:S(2)}) async-start(bf16[32,16,924]{2,1,0:T(8,128)(2,1)} %broadcast_in_dim.19), calls=%async_computation.1 | async-start | bytes 2097152 | tf_op jit(solution)/shard_map/all_to_all | solution.py:16
  52.3 53.0 %all-to-all-start = ((bf16[32,8,512]{2,1,0:T(8,128)(2,1)}), bf16[32,8,512]{2,1,0:T(8,128)(2,1)S(1)}, u32[]{:S(2)}, u32[]{:S(2)}) async-start(bf16[32,8,512]{2,1,0:T(8,128)(2,1)} %broadcast_in_dim.16), calls=%async_computation | async-start | bytes 524288 | tf_op jit(solution)/shard_map/all_to_all | solution.py:16
  130.7 54.3 %all-to-all-start.2 = ((bf16[32,2,14784]{2,1,0:T(2,128)(2,1)}), bf16[32,2,14784]{2,1,0:T(2,128)(2,1)S(1)}, u32[]{:S(2)}, u32[]{:S(2)}) async-start(bf16[32,2,14784]{2,1,0:T(2,128)(2,1)} %reshape.111), calls=%async_computation.2 | async-start | bytes 3801088 | tf_op jit(solution)/shard_map/all_to_all | solution.py:103
  391.7 33.0 %all-to-all-start.3 = ((bf16[16,2,14784]{2,1,0:T(2,128)(2,1)}), bf16[16,2,14784]{2,1,0:T(2,128)(2,1)S(1)}, u32[]{:S(2)}, u32[]{:S(2)}) async-start(bf16[16,2,14784]{2,1,0:T(2,128)(2,1)} %reshape.113), calls=%async_computation.3 | async-start | bytes 1900544 | tf_op jit(solution)/shard_map/all_to_all | solution.py:115
where the time goes:
time: 511 us; the launch traced here: 506 us
  other arithmetic  199 us (39%)
  local copies, waits for them, and re-layouts  118 us (23%)
  blocking collectives  74.7 us (15%)
  waiting for transfers between devices  69.9 us (14%)
  starting transfers between devices  39.9 us (8%)
    unnamed x4, other arithmetic  175 us
    all_to_all x1, waiting for transfers between devices, shards(): lax.all_to_all(product[None], COL, split_axis=1, concat_axis=0, tiled=True)  44.4 us
    psum x4, blocking collectives, one_axis_at_a_time(): shard = lax.psum(shard, axis)  38.3 us
    unnamed x12, local copies, waits for them, and re-layouts  36.5 us
    all_to_all x2, local copies, waits for them, and re-layouts, shards(): lax.all_to_all(decoded[None], ROW, split_axis=2, concat_axis=0, tiled=True)  28.6 us
    all_to_all x1, waiting for transfers between devices, shards(): lax.all_to_all(decoded[None], ROW, split_axis=2, concat_axis=0, tiled=True)  25.5 us
    another operation x2, local copies, waits for them, and re-layouts, shards(): decoded[None]  23.8 us
    all_to_all x2, starting transfers between devices, copy_for_each(): lax.all_to_all(jnp.broadcast_to(shard[None], (peers, *shard.shape)), axis...  23.2 us
  transfers between devices with their start and end apart: 4, of which 2 were waited for; matrix products, arithmetic and copies ran while one was open for 8% of the time, Pallas kernels for 0%

commit v1 on v0

v1 whole, which is shorter than its diff:
```python
import functools

import jax
import jax.numpy as jnp
from jax import lax
from jax.experimental import pallas as pl
from jax.experimental.pallas import tpu as pltpu
from jax.sharding import Mesh
from jax.sharding import PartitionSpec as P

D = 4096
FF = 29568
ROW = ("row_0", "row_1")
COL = ("col_0", "col_1")
ROW_Z = ("row_0", "row_1", "col_1")
N_ROW = 16
N_X = 4
N_Z = 8
N_COL = 32
HALF = FF // N_COL
WIDTH = FF // N_ROW
CHUNK = 64
SHIFT = HALF - (HALF // CHUNK) * CHUNK
BF16 = jnp.bfloat16
F32 = jnp.float32
VMEM_LIMIT = 48 * 1024 * 1024


def low_lanes(rows):
    return lax.broadcasted_iota(jnp.int32, (rows, 128), 1) < 64


def swap_halves(tile):
    return pltpu.roll(tile, 64, 1)


def pack_kernel(half_ref, acts_ref, errs_ref, out_ref, padded):
    padded[...] = jnp.zeros_like(padded)
    padded[:, :HALF] = acts_ref[...].astype(F32)
    plain = padded[...]
    acts = jnp.where(half_ref[0] == 1, pltpu.roll(plain, SHIFT, 1), plain)
    errs = errs_ref[...].astype(F32)
    low = low_lanes(8)
    lane = lax.broadcasted_iota(jnp.int32, (8, 128), 1)
    err_tiles = []
    for z in range(N_Z):
        first = pltpu.roll(errs[:, :128], (128 - 16 * z) % 128, 1)
        second = pltpu.roll(errs[:, 128:], (144 - 16 * z) % 128, 1)
        err_tiles.append(jnp.where(lane < 16, first, second))
    for row in range(N_ROW):
        lanes = slice(128 * (row // 2), 128 * (row // 2) + 128)
        upper, lower = acts[:8, lanes], acts[8:, lanes]
        if row % 2 == 0:
            tile = jnp.where(low, upper, swap_halves(lower))
        else:
            tile = jnp.where(low, swap_halves(upper), lower)
        for z in range(N_Z):
            both = jnp.concatenate([tile, err_tiles[z]], axis=0)
            out_ref[row * N_Z + z] = both.astype(BF16)


def spread_kernel(in_ref, out_ref):
    group = lax.broadcasted_iota(jnp.int32, (64, 128), 1) // 16
    for z in range(N_Z):
        acts = jnp.concatenate(
            [in_ref[row * N_Z + z].astype(F32)[:8] for row in range(N_ROW)], axis=0
        ).astype(BF16)
        for x in range(N_X):
            out_ref[x, 128 * z : 128 * z + 128, :] = acts
    for parity in range(2):
        sums = [jnp.zeros((64, 128), F32) for _ in range(2)]
        for block in range(8):
            row = 2 * block + parity
            source = jnp.concatenate(
                [
                    in_ref[row * N_Z + z].astype(F32)[8:]
                    for z in (0, 2, 4, 6, 1, 3, 5, 7)
                ],
                axis=0,
            )
            for q in range(2):
                turned = pltpu.roll(source, (128 + 16 * (block - q)) % 128, 1)
                sums[q] = jnp.where(group == block, turned, sums[q])
        for q in range(2):
            out_ref[2 * parity + q, 1024:1088, :] = sums[q].astype(BF16)


def node_value(index, count):
    return jnp.cos(jnp.pi * (2.0 * index.astype(F32) + 1.0) / (2.0 * count))


def parity_sign(count):
    return (1 - 2 * (count % 2)).astype(F32)


def mix_kernel(cols_ref, rows_ref, mask_ref, out_ref):
    iota = functools.partial(lax.broadcasted_iota, jnp.int32)
    cols = cols_ref[...]
    rows = rows_ref[...]
    live = mask_ref[...]
    col_eye = iota((N_COL, N_COL), 0) == iota((N_COL, N_COL), 1)
    row_eye = iota((N_ROW, N_ROW), 0) == iota((N_ROW, N_ROW), 1)
    col_point = jnp.sum(jnp.where(col_eye, cols, 0), axis=1, keepdims=True)
    row_point = jnp.sum(jnp.where(row_eye, rows, 0), axis=1, keepdims=True)
    work_acts = node_value(col_point, 2 * N_COL + 1)
    work_errs = node_value(row_point, 2 * N_ROW + 1)
    row_rank = jnp.sum((rows < row_point).astype(jnp.int32), axis=1, keepdims=True)
    row_sign = parity_sign(row_rank)

    lane = iota((1, 128), 1)
    err_in, act_in = lane // 16, lane % 16
    term = parity_sign(err_in) / (work_errs - node_value(err_in, 8))
    total = jnp.sum(jnp.where(act_in == 0, term, 0.0), axis=1, keepdims=True)
    encode_errs = term / total
    term = parity_sign(act_in) / (work_acts - node_value(act_in, 16))
    total = jnp.sum(jnp.where(err_in == 0, term, 0.0), axis=1, keepdims=True)
    encode_acts = term / total
    act_out, err_out = lane // 8, lane % 8
    term = row_sign / (node_value(err_out, 8) - work_errs)
    decode_errs = term / jnp.sum(term, axis=0, keepdims=True)
    inverse = 1.0 / (node_value(act_out, 16) - work_acts)

    lower = cols < col_point
    total = jnp.zeros((128, 128), F32)
    left, right = [], []
    for i in range(N_ROW):
        here = live[i : i + 1, :]
        rank = jnp.sum(jnp.where(lower, here, 0), axis=1, keepdims=True)
        own = jnp.sum(jnp.where(col_eye, here, 0), axis=1, keepdims=True)
        term = (own.astype(F32) * parity_sign(rank)) * inverse
        decode = term / jnp.sum(term, axis=0, keepdims=True)
        left.append(decode * decode_errs[i : i + 1, :])
        right.append(encode_acts * encode_errs[i : i + 1, :])
    total = lax.dot_general(
        jnp.concatenate(left, axis=0),
        jnp.concatenate(right, axis=0),
        (((0,), (0,)), ((), ())),
        preferred_element_type=F32,
        precision=lax.Precision.HIGHEST,
    )
    out_ref[...] = total


def product_kernel(in_ref, mix_ref, out_ref, squares_ref, products):
    low = low_lanes(128)
    errs = jnp.concatenate(
        [
            in_ref[x, 1024 + 32 * part : 1056 + 32 * part, :]
            for part in range(2)
            for x in range(N_X)
        ],
        axis=0,
    )
    errs = errs.astype(F32).T.astype(BF16)
    for block in range(16):
        x, z = block // 4, 2 * (block % 4)
        first = in_ref[x, 128 * z : 128 * z + 128, :].astype(F32)
        second = in_ref[x, 128 * z + 128 : 128 * z + 256, :].astype(F32)
        acts = jnp.concatenate(
            [
                jnp.where(low, first, swap_halves(second)),
                jnp.where(low, swap_halves(first), second),
            ],
            axis=0,
        ).astype(BF16)
        products[pl.ds(block, 128, stride=16), :] = jnp.dot(
            errs, acts, preferred_element_type=F32
        )
    mix = mix_ref[...].astype(BF16)
    squares = jnp.zeros((128, 128), F32)
    for pair in range(8):
        mixed = []
        for r in (2 * pair, 2 * pair + 1):
            piece = jnp.concatenate(
                [
                    products[(block * 16 + r) * 16 : (block * 16 + r) * 16 + 16, :]
                    for block in range(8)
                ],
                axis=0,
            ).astype(BF16)
            grad = jnp.dot(mix, piece, preferred_element_type=F32)
            squares = squares + grad * grad
            mixed.append(grad)
        for k in range(N_ROW):
            both = jnp.concatenate(
                [grad[8 * k : 8 * k + 8, :] for grad in mixed], axis=0
            )
            out_ref[k, 16 * pair : 16 * pair + 16, :] = both.astype(BF16)
    squares_ref[...] = jnp.sum(squares.reshape(16, 8, 128), axis=0)


def place_kernel(in_ref, factor_ref, out_ref, tile_ref):
    low = low_lanes(128)
    factor = factor_ref[0, 0]

    def piece(row):
        return in_ref[row].astype(F32)

    for tile in range(15):
        if tile < 7:
            value = jnp.where(low, piece(2 * tile), swap_halves(piece(2 * tile + 1)))
        elif tile == 7:
            value = jnp.where(low, piece(14) + swap_halves(piece(0)), piece(1))
        elif tile < 14:
            value = jnp.where(
                low, swap_halves(piece(2 * tile - 14)), piece(2 * tile - 13)
            )
        else:
            value = swap_halves(piece(14))
        tile_ref[...] = value * factor
        end = min(128 * tile + 128, WIDTH)
        for l in range(8):
            rows = tile_ref[pl.ds(l, 16, stride=8), :]
            out_ref[l, :, 128 * tile : end] = rows[:, : end - 128 * tile]


def vmem(count):
    return [pl.BlockSpec(memory_space=pltpu.VMEM) for _ in range(count)]


def call(kernel, out, in_specs, scratch=()):
    many = isinstance(out, tuple)
    return pl.pallas_call(
        kernel,
        out_shape=out,
        in_specs=in_specs,
        out_specs=tuple(vmem(len(out))) if many else vmem(1)[0],
        scratch_shapes=list(scratch),
        compiler_params=pltpu.CompilerParams(vmem_limit_bytes=VMEM_LIMIT),
    )


def shards(hidden_acts, output_errors, col_points, row_points, worker_mask):
    shape = jax.ShapeDtypeStruct
    half = (lax.axis_index("col_1") % 2).astype(jnp.int32).reshape(1)
    packed = call(
        pack_kernel,
        shape((N_ROW * N_Z, 16, 128), BF16),
        [pl.BlockSpec(memory_space=pltpu.SMEM)] + vmem(2),
        [pltpu.VMEM((16, 1024), F32)],
    )(half, hidden_acts, output_errors)
    packed = lax.all_to_all(packed, ROW_Z, 0, 0, tiled=True)
    mix = call(mix_kernel, shape((128, 128), F32), vmem(3))(
        col_points[None, :], row_points[None, :], worker_mask
    )
    spread = call(spread_kernel, shape((N_X, 1088, 128), BF16), vmem(1))(packed)
    spread = lax.all_to_all(spread, "col_0", 0, 0, tiled=True)
    mixed, squares = call(
        product_kernel,
        (shape((N_ROW, 128, 128), BF16), shape((8, 128), F32)),
        vmem(2),
        [pltpu.VMEM((2048, 128), F32)],
    )(spread, mix)
    squares = jnp.broadcast_to(jnp.sum(squares), (N_COL, 1, 128))
    squares = jnp.sum(lax.all_to_all(squares, COL, 0, 0, tiled=True)[:, 0, 0])
    squares = jnp.broadcast_to(squares, (N_ROW, 1, 128))
    squares = jnp.sum(lax.all_to_all(squares, ROW, 0, 0, tiled=True)[:, 0, 0])
    mixed = lax.all_to_all(mixed, ROW, 0, 0, tiled=True)
    factor = jnp.minimum(1.0, jnp.sqrt(jnp.float32(FF * D)) / jnp.sqrt(squares + 1e-06))
    return call(
        place_kernel,
        shape((8, 16, WIDTH), F32),
        vmem(1) + [pl.BlockSpec(memory_space=pltpu.SMEM)],
        [pltpu.VMEM((128, 128), F32)],
    )(mixed, factor.reshape(1, 1))


def solution(mesh):
    finer = Mesh(mesh.devices.reshape(8, 2, 4, 8), ROW + COL)
    in_specs = (P(ROW, COL), P(COL, ROW), P(), P(), P())
    return jax.shard_map(
        shards, mesh=finer, in_specs=in_specs, out_specs=P(None, COL, ROW), check_vma=False
    )
```

time: 511 us -> 113 us (0.22)
  other arithmetic: 199 us -> 1.92 us
  local copies, waits for them, and re-layouts: 118 us -> 2.73 us
  waiting for transfers between devices: 69.9 us -> 31.3 us
  starting transfers between devices: 39.9 us -> 8.16 us
  blocking collectives: 74.7 us -> 61.9 us
  Pallas kernels: 0 us -> 5.57 us
    unnamed x4 -> x0, other arithmetic: 175 us -> none
    all_to_all x0 -> x3, blocking collectives: none -> 61.9 us  [the longest x1 39.1 us: shards(): packed = lax.all_to_all(packed, ROW_Z, 0, 0, tiled=True)]
    all_to_all x4 -> x2, waiting for transfers between devices: 69.9 us -> 31.3 us  [the longest x1 16 us: shards(): mixed = lax.all_to_all(mixed, ROW, 0, 0, tiled=True)]
    psum x4 -> x0, blocking collectives: 38.3 us -> none  [one_axis_at_a_time(): shard = lax.psum(shard, axis)]
    all_gather x2 -> x0, blocking collectives: 36.5 us -> none  [the longest x1 18.5 us: shards(): full_errs = lax.all_gather(output_errors, ROW, axis=1, tiled=True)]
    unnamed x12 -> x10, local copies, waits for them, and re-layouts: 36.5 us -> 1.45 us
    all_to_all x4 -> x2, starting transfers between devices: 39.9 us -> 8.16 us  [the longest x1 4.14 us: shards(): spread = lax.all_to_all(spread, 'col_0', 0, 0, tiled=True)]
    all_to_all x2 -> x0, local copies, waits for them, and re-layouts: 28.6 us -> none  [shards(): lax.all_to_all(decoded[None], ROW, split_axis=2, concat_axis=0, tiled=True)]
  transfers between devices with their start and end apart: 4 -> 2, of which waited for: 2 -> 2; matrix products, arithmetic and copies ran while one was open for 8% -> 1% of each run, Pallas kernels for 0% -> 1%
where the time goes in v1:
time: 113 us; the launch traced here: 112 us
  blocking collectives  61.9 us (55%)
  waiting for transfers between devices  31.3 us (28%)
  starting transfers between devices  8.16 us (7%)
  Pallas kernels  5.57 us (5%)
  local copies, waits for them, and re-layouts  2.73 us (2%)
  other arithmetic  1.92 us (2%)
    all_to_all x1, blocking collectives, shards(): packed = lax.all_to_all(packed, ROW_Z, 0, 0, tiled=True)  39.1 us
    all_to_all x1, waiting for transfers between devices, shards(): mixed = lax.all_to_all(mixed, ROW, 0, 0, tiled=True)  16 us
    all_to_all x1, waiting for transfers between devices, shards(): spread = lax.all_to_all(spread, 'col_0', 0, 0, tiled=True)  15.2 us
    all_to_all x1, blocking collectives, shards(): squares = jnp.sum(lax.all_to_all(squares, COL, 0, 0, tiled=True)[:, 0, 0])  11.6 us
    all_to_all x1, blocking collectives, shards(): squares = jnp.sum(lax.all_to_all(squares, ROW, 0, 0, tiled=True)[:, 0, 0])  11.2 us
    all_to_all x1, starting transfers between devices, shards(): spread = lax.all_to_all(spread, 'col_0', 0, 0, tiled=True)  4.14 us
    all_to_all x1, starting transfers between devices, shards(): mixed = lax.all_to_all(mixed, ROW, 0, 0, tiled=True)  4.02 us
  transfers between devices with their start and end apart: 2, of which 2 were waited for; matrix products, arithmetic and copies ran while one was open for 1% of the time, Pallas kernels for 1%

profile of v1, /device:TPU:1, one launch (start us, length us, event | category | flops | bytes accessed | tf_op | source)
XLA Modules:
  0.0 112.3 jit_solution(4981814186074908054)
XLA Ops:
  0.0 0.0 copy-start
  0.0 0.8 copy-done
  0.8 0.0 copy-start.2
  0.8 0.7 copy-done.2
  1.4 0.2 shard_map.55
  1.6 39.1 %all_to_all.25.in_ref = bf16[128,16,128]{2,1,0:T(8,128)(2,1)S(1)} all-to-all(bf16[128,16,128]{2,1,0:T(8,128)(2,1)S(1)} %shard_map.55), channel_id=1, replica_groups=mesh['row_0'=8,'row_1'=2,'col_0'=4,'col_1'=8] {'row_0','row_1','col_1'}, dimensions={0} | all-to-all | bytes 1048576 | tf_op jit(solution)/shard_map/all_to_all | solution.py:242
  40.8 1.3 %shard_map.56 = bf16[4,1088,128]{2,1,0:T(8,128)(2,1)} custom-call(bf16[128,16,128]{2,1,0:T(8,128)(2,1)S(1)} %all_to_all.25.in_ref), custom_call_target="tpu_custom_call" | custom-call | tf_op jit(solution)/shard_map/pallas_call | solution.py:246
  42.0 0.0 copy-start.1
  42.0 0.0 copy-start.3
  42.0 0.0 copy-start.4
  42.0 4.1 %all-to-all-start.1 = ((bf16[4,1088,128]{2,1,0:T(8,128)(2,1)}), bf16[4,1088,128]{2,1,0:T(8,128)(2,1)S(1)}, u32[]{:S(2)}, u32[]{:S(2)}) async-start(bf16[4,1088,128]{2,1,0:T(8,128)(2,1)} %shard_map.56), calls=%async_computation.1 | async-start | bytes 2228224 | tf_op jit(solution)/shard_map/all_to_all | solution.py:247
  46.2 0.0 copy-done.1
  46.2 0.0 copy-done.3
  46.2 0.0 copy-done.4
  46.2 1.0 shard_map.57.mix_ref
  47.2 15.2 %all-to-all-done.1.in_ref = bf16[4,1088,128]{2,1,0:T(8,128)(2,1)S(1)} async-done(((bf16[4,1088,128]{2,1,0:T(8,128)(2,1)}), bf16[4,1088,128]{2,1,0:T(8,128)(2,1)S(1)}, u32[]{:S(2)}, u32[]{:S(2)}) %all-to-all-start.1) | async-done | bytes 1114144 | tf_op jit(solution)/shard_map/all_to_all | solution.py:247
  62.5 1.8 %shard_map.58 = (bf16[16,128,128]{2,1,0:T(8,128)(2,1)}, f32[8,128]{1,0:T(8,128)S(1)}) custom-call(bf16[4,1088,128]{2,1,0:T(8,128)(2,1)S(1)} %all-to-all-done.1.in_ref, f32[128,128]{1,0:T(8,128)S(1)} %shard_map.57.mix_ref), custom_call_target="tpu_custom_call" | custom-call | tf_op jit(solution)/shard_map/pallas_call | solution.py:248
  64.3 0.6 reduce_sum.27
  64.9 0.6 broadcast_in_dim.14
  65.6 11.6 %all_to_all.26 = f32[32,1,128]{2,1,0:T(1,128)S(1)} all-to-all(f32[32,1,128]{2,1,0:T(1,128)S(1)} %broadcast_in_dim.14), channel_id=1, replica_groups=mesh['row_0'=8,'row_1'=2,'col_0'=4,'col_1'=8] {'col_0','col_1'}, dimensions={0} | all-to-all | bytes 32768 | tf_op jit(solution)/shard_map/all_to_all | solution.py:255
  77.2 0.7 slice_reduce_fusion
  77.9 0.6 broadcast_in_dim.15
  78.5 11.2 %all_to_all.27 = f32[16,1,128]{2,1,0:T(1,128)S(1)} all-to-all(f32[16,1,128]{2,1,0:T(1,128)S(1)} %broadcast_in_dim.15), channel_id=1, replica_groups=mesh['row_0'=8,'row_1'=2,'col_0'=4,'col_1'=8] {'row_0','row_1'}, dimensions={0} | all-to-all | bytes 16384 | tf_op jit(solution)/shard_map/all_to_all | solution.py:257
  89.7 4.0 %all-to-all-start.2 = ((bf16[16,128,128]{2,1,0:T(8,128)(2,1)}), bf16[16,128,128]{2,1,0:T(8,128)(2,1)S(1)}, u32[]{:S(2)}, u32[]{:S(2)}) async-start(bf16[16,128,128]{2,1,0:T(8,128)(2,1)} %get-tuple-element.7), calls=%async_computation.2 | async-start | bytes 1048576 | tf_op jit(solution)/shard_map/all_to_all | solution.py:258
  93.7 0.6 slice_reduce_fusion.1
  95.0 16.0 %all-to-all-done.2.in_ref = bf16[16,128,128]{2,1,0:T(8,128)(2,1)S(1)} async-done(((bf16[16,128,128]{2,1,0:T(8,128)(2,1)}), bf16[16,128,128]{2,1,0:T(8,128)(2,1)S(1)}, u32[]{:S(2)}, u32[]{:S(2)}) %all-to-all-start.2) | async-done | bytes 524320 | tf_op jit(solution)/shard_map/all_to_all | solution.py:258
  111.1 1.2 %shard_map.59 = f32[8,16,1848]{2,1,0:T(8,128)} custom-call(bf16[16,128,128]{2,1,0:T(8,128)(2,1)S(1)} %all-to-all-done.2.in_ref, f32[1,1]{1,0:T(1,128)} %bitcast.3.factor_ref), custom_call_target="tpu_custom_call" | custom-call | tf_op jit(solution)/shard_map/pallas_call | solution.py:260
Async XLA Ops:
  0.0 0.8 copy-start
  0.8 0.7 copy-start.2
  42.0 4.2 %copy-start.1 = (s32[16,32]{1,0:T(8,128)S(1)}, s32[16,32]{1,0:T(8,128)}, u32[]{:S(2)}) copy-start(s32[16,32]{1,0:T(8,128)} %mask_ref.1) | copy-start | bytes 6148
  42.0 4.2 %copy-start.3 = (s32[32]{0:T(128)S(1)}, s32[32]{0:T(128)}, u32[]{:S(2)}) copy-start(s32[32]{0:T(128)} %param.7) | copy-start | bytes 388
  42.0 4.2 %copy-start.4 = (s32[16]{0:T(128)S(1)}, s32[16]{0:T(128)}, u32[]{:S(2)}) copy-start(s32[16]{0:T(128)} %param.8) | copy-start | bytes 196
  42.0 20.4 %all-to-all-start.1 = ((bf16[4,1088,128]{2,1,0:T(8,128)(2,1)}), bf16[4,1088,128]{2,1,0:T(8,128)(2,1)S(1)}, u32[]{:S(2)}, u32[]{:S(2)}) async-start(bf16[4,1088,128]{2,1,0:T(8,128)(2,1)} %shard_map.56), calls=%async_computation.1 | async-start | bytes 2228224 | tf_op jit(solution)/shard_map/all_to_all | solution.py:247
  89.7 21.4 %all-to-all-start.2 = ((bf16[16,128,128]{2,1,0:T(8,128)(2,1)}), bf16[16,128,128]{2,1,0:T(8,128)(2,1)S(1)}, u32[]{:S(2)}, u32[]{:S(2)}) async-start(bf16[16,128,128]{2,1,0:T(8,128)(2,1)} %get-tuple-element.7), calls=%async_computation.2 | async-start | bytes 1048576 | tf_op jit(solution)/shard_map/all_to_all | solution.py:258

commit v2 on v1

--- a/solution.py
+++ b/solution.py
@@ -34,19 +34,26 @@
     return pltpu.roll(tile, 64, 1)
 
 
-def pack_kernel(half_ref, acts_ref, errs_ref, out_ref, padded):
+def pack_kernel(acts_ref, errs_ref, out_ref, padded, packed):
     padded[...] = jnp.zeros_like(padded)
     padded[:, :HALF] = acts_ref[...].astype(F32)
     plain = padded[...]
-    acts = jnp.where(half_ref[0] == 1, pltpu.roll(plain, SHIFT, 1), plain)
+    second_half = lax.rem(lax.axis_index("col_1"), 2) == 1
+    acts = jnp.where(second_half, pltpu.roll(plain, SHIFT, 1), plain)
     errs = errs_ref[...].astype(F32)
     low = low_lanes(8)
     lane = lax.broadcasted_iota(jnp.int32, (8, 128), 1)
+    quarter = lane[:2] // 32
     err_tiles = []
     for z in range(N_Z):
         first = pltpu.roll(errs[:, :128], (128 - 16 * z) % 128, 1)
         second = pltpu.roll(errs[:, 128:], (144 - 16 * z) % 128, 1)
-        err_tiles.append(jnp.where(lane < 16, first, second))
+        both = jnp.where(lane < 16, first, second)
+        tile = both[:2]
+        for v in range(1, 4):
+            turned = pltpu.roll(both, 32 * v, 1)
+            tile = jnp.where(quarter == v, turned[2 * v : 2 * v + 2], tile)
+        err_tiles.append(tile)
     for row in range(N_ROW):
         lanes = slice(128 * (row // 2), 128 * (row // 2) + 128)
         upper, lower = acts[:8, lanes], acts[8:, lanes]
@@ -55,34 +62,44 @@
         else:
             tile = jnp.where(low, swap_halves(upper), lower)
         for z in range(N_Z):
-            both = jnp.concatenate([tile, err_tiles[z]], axis=0)
-            out_ref[row * N_Z + z] = both.astype(BF16)
-
-
-def spread_kernel(in_ref, out_ref):
-    group = lax.broadcasted_iota(jnp.int32, (64, 128), 1) // 16
+            start = (row * N_Z + z) * 10
+            packed[start : start + 8, :] = tile
+            packed[start + 8 : start + 10, :] = err_tiles[z]
+    out_ref[...] = packed[...].astype(BF16)
+
+
+def spread_kernel(in_ref, out_ref, packed):
+    packed[...] = in_ref[...].astype(F32)
+    group = lax.broadcasted_iota(jnp.int32, (8, 128), 1) // 16
     for z in range(N_Z):
-        acts = jnp.concatenate(
-            [in_ref[row * N_Z + z].astype(F32)[:8] for row in range(N_ROW)], axis=0
-        ).astype(BF16)
+        starts = [(row * N_Z + z) * 10 for row in range(N_ROW)]
+        acts = jnp.concatenate([packed[s : s + 8, :] for s in starts], axis=0)
+        acts = acts.astype(BF16)
         for x in range(N_X):
             out_ref[x, 128 * z : 128 * z + 128, :] = acts
     for parity in range(2):
-        sums = [jnp.zeros((64, 128), F32) for _ in range(2)]
+        sums = [[jnp.zeros((8, 128), F32) for _ in range(8)] for _ in range(2)]
         for block in range(8):
-            row = 2 * block + parity
-            source = jnp.concatenate(
-                [
-                    in_ref[row * N_Z + z].astype(F32)[8:]
-                    for z in (0, 2, 4, 6, 1, 3, 5, 7)
-                ],
-                axis=0,
-            )
-            for q in range(2):
-                turned = pltpu.roll(source, (128 + 16 * (block - q)) % 128, 1)
-                sums[q] = jnp.where(group == block, turned, sums[q])
+            for part in range(2):
+                starts = [
+                    ((2 * block + parity) * N_Z + z) * 10 + 8
+                    for z in range(part, N_Z, 2)
+                ]
+                source = jnp.concatenate(
+                    [packed[s : s + 2, :] for s in starts], axis=0
+                )
+                for v in range(4):
+                    for q in range(2):
+                        turned = pltpu.roll(
+                            source, (128 + 16 * (block - q) - 32 * v) % 128, 1
+                        )
+                        place = 4 * part + v
+                        sums[q][place] = jnp.where(
+                            group == block, turned, sums[q][place]
+                        )
         for q in range(2):
-            out_ref[2 * parity + q, 1024:1088, :] = sums[q].astype(BF16)
+            errs = jnp.concatenate(sums[q], axis=0).astype(BF16)
+            out_ref[2 * parity + q, 1024:1088, :] = errs
 
 
 def node_value(index, count):
@@ -121,7 +138,6 @@
     inverse = 1.0 / (node_value(act_out, 16) - work_acts)
 
     lower = cols < col_point
-    total = jnp.zeros((128, 128), F32)
     left, right = [], []
     for i in range(N_ROW):
         here = live[i : i + 1, :]
@@ -138,7 +154,7 @@
         preferred_element_type=F32,
         precision=lax.Precision.HIGHEST,
     )
-    out_ref[...] = total
+    out_ref[...] = total.astype(BF16)
 
 
 def product_kernel(in_ref, mix_ref, out_ref, squares_ref, products):
@@ -151,7 +167,15 @@
         ],
         axis=0,
     )
-    errs = errs.astype(F32).T.astype(BF16)
+    here = lax.broadcasted_iota(jnp.int32, (256, 256), 0)
+    there = lax.broadcasted_iota(jnp.int32, (256, 256), 1)
+    source = there // 32 * 32 + there // 2 % 4 * 8 + there // 8 % 4 * 2 + there % 2
+    errs = lax.dot_general(
+        errs,
+        jnp.where(here == source, 1.0, 0.0).astype(BF16),
+        (((0,), (0,)), ((), ())),
+        preferred_element_type=F32,
+    ).astype(BF16)
     for block in range(16):
         x, z = block // 4, 2 * (block % 4)
         first = in_ref[x, 128 * z : 128 * z + 128, :].astype(F32)
@@ -166,7 +190,7 @@
         products[pl.ds(block, 128, stride=16), :] = jnp.dot(
             errs, acts, preferred_element_type=F32
         )
-    mix = mix_ref[...].astype(BF16)
+    mix = mix_ref[...]
     squares = jnp.zeros((128, 128), F32)
     for pair in range(8):
         mixed = []
@@ -186,15 +210,31 @@
                 [grad[8 * k : 8 * k + 8, :] for grad in mixed], axis=0
             )
             out_ref[k, 16 * pair : 16 * pair + 16, :] = both.astype(BF16)
-    squares_ref[...] = jnp.sum(squares.reshape(16, 8, 128), axis=0)
-
-
-def place_kernel(in_ref, factor_ref, out_ref, tile_ref):
+    squares_ref[...] = jnp.full(squares_ref.shape, jnp.sum(squares), F32)
+
+
+def carry_kernel(in_ref, squares_ref, out_ref):
+    out_ref[:, :128, :] = in_ref[...]
+    total = jnp.sum(squares_ref[...], axis=0)
+    high = total.astype(BF16).astype(F32)
+    middle = (total - high).astype(BF16).astype(F32)
+    row = lax.broadcasted_iota(jnp.int32, (8, 128), 0)
+    rows = jnp.where(row == 0, high, jnp.where(row == 1, middle, total - high - middle))
+    rows = jnp.where(row < 3, rows, 0.0).astype(BF16)
+    for k in range(N_ROW):
+        out_ref[k, 128:136, :] = rows
+
+
+def place_kernel(in_ref, out_ref, tile_ref):
     low = low_lanes(128)
-    factor = factor_ref[0, 0]
+    squares = jnp.zeros((8, 128), F32)
+    for row in range(N_ROW):
+        squares = squares + in_ref[row, 128:136, :].astype(F32)
+    squares = jnp.sum(squares, axis=0, keepdims=True)
+    factor = jnp.minimum(1.0, jnp.sqrt(jnp.float32(FF * D)) / jnp.sqrt(squares + 1e-06))
 
     def piece(row):
-        return in_ref[row].astype(F32)
+        return in_ref[row, :128, :].astype(F32)
 
     for tile in range(15):
         if tile < 7:
@@ -232,37 +272,42 @@
 
 def shards(hidden_acts, output_errors, col_points, row_points, worker_mask):
     shape = jax.ShapeDtypeStruct
-    half = (lax.axis_index("col_1") % 2).astype(jnp.int32).reshape(1)
     packed = call(
         pack_kernel,
-        shape((N_ROW * N_Z, 16, 128), BF16),
-        [pl.BlockSpec(memory_space=pltpu.SMEM)] + vmem(2),
-        [pltpu.VMEM((16, 1024), F32)],
-    )(half, hidden_acts, output_errors)
+        shape((N_ROW * N_Z * 10, 128), BF16),
+        vmem(2),
+        [
+            pltpu.VMEM((16, 1024), F32),
+            pltpu.VMEM((N_ROW * N_Z * 10, 128), F32),
+        ],
+    )(hidden_acts, output_errors)
+    mix = call(mix_kernel, shape((128, 128), BF16), vmem(3))(
+        col_points[None, :], row_points[None, :], worker_mask
+    )
+    packed = packed.reshape(N_ROW * N_Z, 5, 2, 128)
     packed = lax.all_to_all(packed, ROW_Z, 0, 0, tiled=True)
-    mix = call(mix_kernel, shape((128, 128), F32), vmem(3))(
-        col_points[None, :], row_points[None, :], worker_mask
-    )
-    spread = call(spread_kernel, shape((N_X, 1088, 128), BF16), vmem(1))(packed)
+    spread = call(
+        spread_kernel,
+        shape((N_X, 1088, 128), BF16),
+        vmem(1),
+        [pltpu.VMEM((N_ROW * N_Z * 10, 128), F32)],
+    )(packed.reshape(N_ROW * N_Z * 10, 128))
     spread = lax.all_to_all(spread, "col_0", 0, 0, tiled=True)
     mixed, squares = call(
         product_kernel,
-        (shape((N_ROW, 128, 128), BF16), shape((8, 128), F32)),
+        (shape((N_ROW, 128, 128), BF16), shape((N_COL, 1, 128), F32)),
         vmem(2),
         [pltpu.VMEM((2048, 128), F32)],
     )(spread, mix)
-    squares = jnp.broadcast_to(jnp.sum(squares), (N_COL, 1, 128))
-    squares = jnp.sum(lax.all_to_all(squares, COL, 0, 0, tiled=True)[:, 0, 0])
-    squares = jnp.broadcast_to(squares, (N_ROW, 1, 128))
-    squares = jnp.sum(lax.all_to_all(squares, ROW, 0, 0, tiled=True)[:, 0, 0])
+    squares = lax.all_to_all(squares, COL, 0, 0, tiled=True)
+    mixed = call(carry_kernel, shape((N_ROW, 136, 128), BF16), vmem(2))(mixed, squares)
     mixed = lax.all_to_all(mixed, ROW, 0, 0, tiled=True)
-    factor = jnp.minimum(1.0, jnp.sqrt(jnp.float32(FF * D)) / jnp.sqrt(squares + 1e-06))
     return call(
         place_kernel,
         shape((8, 16, WIDTH), F32),
-        vmem(1) + [pl.BlockSpec(memory_space=pltpu.SMEM)],
+        vmem(1),
         [pltpu.VMEM((128, 128), F32)],
-    )(mixed, factor.reshape(1, 1))
+    )(mixed)
 
 
 def solution(mesh):

time: 113 us -> 95.8 us (0.85)
  waiting for transfers between devices: 31.3 us -> 15.2 us
  blocking collectives: 61.9 us -> 69.3 us
  starting transfers between devices: 8.16 us -> 4.14 us
  other arithmetic: 1.92 us -> 0 us
  local copies, waits for them, and re-layouts: 2.73 us -> 1.45 us
    all_to_all x1 -> x0, waiting for transfers between devices: 16 us -> none  [shards(): mixed = lax.all_to_all(mixed, ROW, 0, 0, tiled=True)]
    all_to_all x2, blocking collectives: 22.8 us -> 34.4 us  [the longest x1 22.8 us: shards(): mixed = lax.all_to_all(mixed, ROW, 0, 0, tiled=True)]
    all_to_all x1, blocking collectives: 39.1 us -> 34.9 us  [shards(): packed = lax.all_to_all(packed, ROW_Z, 0, 0, tiled=True)]
    all_to_all x1 -> x0, starting transfers between devices: 4.02 us -> none  [shards(): mixed = lax.all_to_all(mixed, ROW, 0, 0, tiled=True)]
    reduce_sum x3 -> x0, other arithmetic: 1.92 us -> none  [the longest x1 0.66 us: shards(): squares = jnp.sum(lax.all_to_all(squares, COL, 0, 0, tiled=True)[:, 0, 0])]
    broadcast_in_dim x2 -> x0, local copies, waits for them, and re-layouts: 1.28 us -> none  [the longest x1 0.64 us: shards(): squares = jnp.broadcast_to(jnp.sum(squares), (N_COL, 1, 128))]
    pallas_call x5 -> x6, Pallas kernels: 5.57 us -> 5.16 us  [the longest x1 1.29 us: shards(): call(product_kernel, (shape((N_ROW, 128, 128), BF16), shape((N_COL, 1, 12...]
  transfers between devices with their start and end apart: 2 -> 1, of which waited for: 2 -> 1; matrix products, arithmetic and copies ran while one was open for 1% -> 0% of each run, Pallas kernels for 1% -> 1%
where the time goes in v2:
time: 95.8 us; the launch traced here: 95.4 us
  blocking collectives  69.3 us (72%)
  waiting for transfers between devices  15.2 us (16%)
  Pallas kernels  5.16 us (5%)
  starting transfers between devices  4.14 us (4%)
  local copies, waits for them, and re-layouts  1.45 us (2%)
    all_to_all x1, blocking collectives, shards(): packed = lax.all_to_all(packed, ROW_Z, 0, 0, tiled=True)  34.9 us
    all_to_all x1, blocking collectives, shards(): mixed = lax.all_to_all(mixed, ROW, 0, 0, tiled=True)  22.8 us
    all_to_all x1, waiting for transfers between devices, shards(): spread = lax.all_to_all(spread, 'col_0', 0, 0, tiled=True)  15.2 us
    all_to_all x1, blocking collectives, shards(): squares = lax.all_to_all(squares, COL, 0, 0, tiled=True)  11.6 us
    all_to_all x1, starting transfers between devices, shards(): spread = lax.all_to_all(spread, 'col_0', 0, 0, tiled=True)  4.14 us
  transfers between devices with their start and end apart: 1, of which 1 were waited for; matrix products, arithmetic and copies ran while one was open for 0% of the time, Pallas kernels for 1%

profile of v2, /device:TPU:1, one launch (start us, length us, event | category | flops | bytes accessed | tf_op | source)
XLA Modules:
  0.0 95.4 jit_solution(2807960865419229872)
XLA Ops:
  0.0 0.0 copy-start
  0.0 0.8 copy-done
  0.8 0.0 copy-start.2
  0.8 0.7 copy-done.2
  1.4 0.2 shard_map.55
  1.7 34.9 %all_to_all.20 = bf16[128,5,2,128]{3,2,1,0:T(2,128)(2,1)S(1)} all-to-all(bf16[128,5,2,128]{3,2,1,0:T(2,128)(2,1)S(1)} %bitcast.4), channel_id=1, replica_groups=mesh['row_0'=8,'row_1'=2,'col_0'=4,'col_1'=8] {'row_0','row_1','col_1'}, dimensions={0} | all-to-all | bytes 655360 | tf_op jit(solution)/shard_map/all_to_all | solution.py:288
  36.6 1.3 %shard_map.56 = bf16[4,1088,128]{2,1,0:T(8,128)(2,1)} custom-call(bf16[1280,128]{1,0:T(8,128)(2,1)S(1)} %bitcast.5), custom_call_target="tpu_custom_call" | custom-call | tf_op jit(solution)/shard_map/pallas_call | solution.py:289
  37.9 0.0 copy-start.1
  37.9 0.0 copy-start.3
  37.9 0.0 copy-start.4
  37.9 4.1 %all-to-all-start.1 = ((bf16[4,1088,128]{2,1,0:T(8,128)(2,1)}), bf16[4,1088,128]{2,1,0:T(8,128)(2,1)S(1)}, u32[]{:S(2)}, u32[]{:S(2)}) async-start(bf16[4,1088,128]{2,1,0:T(8,128)(2,1)} %shard_map.56), calls=%async_computation.1 | async-start | bytes 2228224 | tf_op jit(solution)/shard_map/all_to_all | solution.py:295
  42.1 0.0 copy-done.1
  42.1 0.0 copy-done.3
  42.1 0.0 copy-done.4
  42.1 1.0 %shard_map.57.mix_ref = bf16[128,128]{1,0:T(8,128)(2,1)S(1)} custom-call(s32[1,32]{1,0:T(1,128)S(1)} %bitcast.6, s32[1,16]{1,0:T(1,128)S(1)} %bitcast.7, s32[16,32]{1,0:T(8,128)S(1)} %copy-done.1), custom_call_target="tpu_custom_call" | custom-call | tf_op jit(solution)/shard_map/pallas_call | solution.py:284
  43.1 15.2 %all-to-all-done.1.in_ref = bf16[4,1088,128]{2,1,0:T(8,128)(2,1)S(1)} async-done(((bf16[4,1088,128]{2,1,0:T(8,128)(2,1)}), bf16[4,1088,128]{2,1,0:T(8,128)(2,1)S(1)}, u32[]{:S(2)}, u32[]{:S(2)}) %all-to-all-start.1) | async-done | bytes 1114144 | tf_op jit(solution)/shard_map/all_to_all | solution.py:295
  58.3 1.3 %shard_map.58 = (bf16[16,128,128]{2,1,0:T(8,128)(2,1)S(1)}, f32[32,1,128]{2,1,0:T(1,128)S(1)}) custom-call(bf16[4,1088,128]{2,1,0:T(8,128)(2,1)S(1)} %all-to-all-done.1.in_ref, bf16[128,128]{1,0:T(8,128)(2,1)S(1)} %shard_map.57.mix_ref), custom_call_target="tpu_custom_call" | custom-call | tf_op jit(solution)/shard_map/pallas_call | solution.py:296
  59.6 11.6 %all_to_all.21.squares_ref = f32[32,1,128]{2,1,0:T(1,128)S(1)} all-to-all(f32[32,1,128]{2,1,0:T(1,128)S(1)} %get-tuple-element.8), channel_id=1, replica_groups=mesh['row_0'=8,'row_1'=2,'col_0'=4,'col_1'=8] {'col_0','col_1'}, dimensions={0} | all-to-all | bytes 32768 | tf_op jit(solution)/shard_map/all_to_all | solution.py:302
  71.3 0.1 shard_map.59
  71.3 22.8 %all_to_all.22.in_ref = bf16[16,136,128]{2,1,0:T(8,128)(2,1)S(1)} all-to-all(bf16[16,136,128]{2,1,0:T(8,128)(2,1)S(1)} %shard_map.59), channel_id=1, replica_groups=mesh['row_0'=8,'row_1'=2,'col_0'=4,'col_1'=8] {'row_0','row_1'}, dimensions={0} | all-to-all | bytes 1114112 | tf_op jit(solution)/shard_map/all_to_all | solution.py:304
  94.1 1.2 %shard_map.60 = f32[8,16,1848]{2,1,0:T(8,128)} custom-call(bf16[16,136,128]{2,1,0:T(8,128)(2,1)S(1)} %all_to_all.22.in_ref), custom_call_target="tpu_custom_call" | custom-call | tf_op jit(solution)/shard_map/pallas_call | solution.py:305
Async XLA Ops:
  0.0 0.8 copy-start
  0.8 0.7 copy-start.2
  37.9 4.2 %copy-start.1 = (s32[16,32]{1,0:T(8,128)S(1)}, s32[16,32]{1,0:T(8,128)}, u32[]{:S(2)}) copy-start(s32[16,32]{1,0:T(8,128)} %mask_ref.1) | copy-start | bytes 6148
  37.9 4.2 %copy-start.3 = (s32[32]{0:T(128)S(1)}, s32[32]{0:T(128)}, u32[]{:S(2)}) copy-start(s32[32]{0:T(128)} %param.7) | copy-start | bytes 388
  37.9 4.2 %copy-start.4 = (s32[16]{0:T(128)S(1)}, s32[16]{0:T(128)}, u32[]{:S(2)}) copy-start(s32[16]{0:T(128)} %param.8) | copy-start | bytes 196
  37.9 20.4 %all-to-all-start.1 = ((bf16[4,1088,128]{2,1,0:T(8,128)(2,1)}), bf16[4,1088,128]{2,1,0:T(8,128)(2,1)S(1)}, u32[]{:S(2)}, u32[]{:S(2)}) async-start(bf16[4,1088,128]{2,1,0:T(8,128)(2,1)} %shard_map.56), calls=%async_computation.1 | async-start | bytes 2228224 | tf_op jit(solution)/shard_map/all_to_all | solution.py:295

commit v3 on v2

--- a/solution.py
+++ b/solution.py
@@ -12,6 +12,7 @@
 FF = 29568
 ROW = ("row_0", "row_1")
 COL = ("col_0", "col_1")
+ROW_X = ("row_0", "row_1", "col_0")
 ROW_Z = ("row_0", "row_1", "col_1")
 N_ROW = 16
 N_X = 4
@@ -42,6 +43,7 @@
     acts = jnp.where(second_half, pltpu.roll(plain, SHIFT, 1), plain)
     errs = errs_ref[...].astype(F32)
     low = low_lanes(8)
+    up = 32 * lax.div(lax.axis_index("col_1"), 2)
     lane = lax.broadcasted_iota(jnp.int32, (8, 128), 1)
     quarter = lane[:2] // 32
     err_tiles = []
@@ -61,6 +63,7 @@
             tile = jnp.where(low, upper, swap_halves(lower))
         else:
             tile = jnp.where(low, swap_halves(upper), lower)
+        tile = pltpu.roll(tile, up, 1)
         for z in range(N_Z):
             start = (row * N_Z + z) * 10
             packed[start : start + 8, :] = tile
@@ -68,15 +71,31 @@
     out_ref[...] = packed[...].astype(BF16)
 
 
+def gather_group(tiles, which):
+    rows = tiles[0].shape[0]
+    wanted = lax.broadcasted_iota(jnp.int32, (rows, 128), 1) // 32
+    result = tiles[-which % 4]
+    for place in range(1, 4):
+        result = jnp.where(wanted == place, tiles[(place - which) % 4], result)
+    return pltpu.roll(result, 128 - 32 * which, 1) if which else result
+
+
 def spread_kernel(in_ref, out_ref, packed):
     packed[...] = in_ref[...].astype(F32)
     group = lax.broadcasted_iota(jnp.int32, (8, 128), 1) // 16
-    for z in range(N_Z):
-        starts = [(row * N_Z + z) * 10 for row in range(N_ROW)]
-        acts = jnp.concatenate([packed[s : s + 8, :] for s in starts], axis=0)
-        acts = acts.astype(BF16)
-        for x in range(N_X):
-            out_ref[x, 128 * z : 128 * z + 128, :] = acts
+    for pair in range(N_ROW // 2):
+        for half in range(2):
+            sources = []
+            for row in (2 * pair, 2 * pair + 1):
+                starts = [(row * N_Z + z) * 10 for z in range(half, N_Z, 2)]
+                sources.append([packed[s : s + 8, :] for s in starts])
+            for part in range(2):
+                for q in range(2):
+                    both = jnp.concatenate(
+                        [gather_group(tiles, 2 * part + q) for tiles in sources], axis=0
+                    )
+                    start = 128 * part + 16 * pair
+                    out_ref[2 * half + q, start : start + 16, :] = both.astype(BF16)
     for parity in range(2):
         sums = [[jnp.zeros((8, 128), F32) for _ in range(8)] for _ in range(2)]
         for block in range(8):
@@ -99,7 +118,9 @@
                         )
         for q in range(2):
             errs = jnp.concatenate(sums[q], axis=0).astype(BF16)
-            out_ref[2 * parity + q, 1024:1088, :] = errs
+            start = 256 + 64 * (2 * parity + q)
+            for x in range(N_X):
+                out_ref[x, start : start + 64, :] = errs
 
 
 def node_value(index, count):
@@ -157,100 +178,100 @@
     out_ref[...] = total.astype(BF16)
 
 
+def one_hot(source, size):
+    here = lax.broadcasted_iota(jnp.int32, (size, size), 0)
+    return jnp.where(here == source, 1.0, 0.0).astype(BF16)
+
+
 def product_kernel(in_ref, mix_ref, out_ref, squares_ref, products):
-    low = low_lanes(128)
-    errs = jnp.concatenate(
-        [
-            in_ref[x, 1024 + 32 * part : 1056 + 32 * part, :]
-            for part in range(2)
-            for x in range(N_X)
-        ],
-        axis=0,
-    )
-    here = lax.broadcasted_iota(jnp.int32, (256, 256), 0)
-    there = lax.broadcasted_iota(jnp.int32, (256, 256), 1)
-    source = there // 32 * 32 + there // 2 % 4 * 8 + there // 8 % 4 * 2 + there % 2
-    errs = lax.dot_general(
-        errs,
-        jnp.where(here == source, 1.0, 0.0).astype(BF16),
-        (((0,), (0,)), ((), ())),
-        preferred_element_type=F32,
-    ).astype(BF16)
-    for block in range(16):
-        x, z = block // 4, 2 * (block % 4)
-        first = in_ref[x, 128 * z : 128 * z + 128, :].astype(F32)
-        second = in_ref[x, 128 * z + 128 : 128 * z + 256, :].astype(F32)
-        acts = jnp.concatenate(
+    to = lax.broadcasted_iota(jnp.int32, (256, 256), 1)
+    tokens = one_hot(
+        to // 32 * 32 + to // 2 % 4 * 8 + to // 8 % 4 * 2 + to % 2, 256
+    )
+    to = lax.broadcasted_iota(jnp.int32, (128, 128), 1)
+    up = 2 * lax.axis_index("row_1") + lax.rem(lax.axis_index("col_0"), 2)
+    features = one_hot(to % 8 * 16 + to // 8 % 4 * 4 + (to // 32 + 4 - up) % 4, 128)
+    turned = []
+    for target in range(N_X):
+        errs = jnp.concatenate(
             [
-                jnp.where(low, first, swap_halves(second)),
-                jnp.where(low, swap_halves(first), second),
+                in_ref[x, start : start + 32, :]
+                for start in (256 + 64 * target, 288 + 64 * target)
+                for x in range(N_X)
             ],
             axis=0,
-        ).astype(BF16)
-        products[pl.ds(block, 128, stride=16), :] = jnp.dot(
-            errs, acts, preferred_element_type=F32
         )
+        errs = jnp.dot(errs, features, preferred_element_type=F32).astype(BF16)
+        turned.append(
+            lax.dot_general(
+                errs, tokens, (((0,), (0,)), ((), ())), preferred_element_type=F32
+            ).astype(BF16)
+        )
+    errs = jnp.concatenate(
+        [tile[32 * r : 32 * r + 32, :] for r in range(4) for tile in turned], axis=0
+    )
+    for x in range(N_X):
+        product = jnp.dot(errs, in_ref[x, :256, :], preferred_element_type=F32)
+        tiles = [product[128 * r : 128 * r + 128, :] for r in range(4)]
+        tiles = [pltpu.roll(tile, 32 * r, 1) if r else tile for r, tile in enumerate(tiles)]
+        for i in range(4):
+            products[pl.ds(4 * x + i, 128, stride=16), :] = gather_group(tiles, i)
     mix = mix_ref[...]
     squares = jnp.zeros((128, 128), F32)
     for pair in range(8):
         mixed = []
-        for r in (2 * pair, 2 * pair + 1):
-            piece = jnp.concatenate(
-                [
-                    products[(block * 16 + r) * 16 : (block * 16 + r) * 16 + 16, :]
-                    for block in range(8)
-                ],
-                axis=0,
-            ).astype(BF16)
+        for s in (2 * pair, 2 * pair + 1):
+            piece = products[128 * s : 128 * s + 128, :].astype(BF16)
             grad = jnp.dot(mix, piece, preferred_element_type=F32)
             squares = squares + grad * grad
             mixed.append(grad)
+        start = 16 * (pair % 2)
         for k in range(N_ROW):
             both = jnp.concatenate(
                 [grad[8 * k : 8 * k + 8, :] for grad in mixed], axis=0
             )
-            out_ref[k, 16 * pair : 16 * pair + 16, :] = both.astype(BF16)
+            out_ref[N_X * k + pair // 2, start : start + 16, :] = both.astype(BF16)
     squares_ref[...] = jnp.full(squares_ref.shape, jnp.sum(squares), F32)
 
 
-def carry_kernel(in_ref, squares_ref, out_ref):
-    out_ref[:, :128, :] = in_ref[...]
+def carry_kernel(in_ref, squares_ref, out_ref, packed):
     total = jnp.sum(squares_ref[...], axis=0)
     high = total.astype(BF16).astype(F32)
     middle = (total - high).astype(BF16).astype(F32)
-    row = lax.broadcasted_iota(jnp.int32, (8, 128), 0)
-    rows = jnp.where(row == 0, high, jnp.where(row == 1, middle, total - high - middle))
-    rows = jnp.where(row < 3, rows, 0.0).astype(BF16)
-    for k in range(N_ROW):
-        out_ref[k, 128:136, :] = rows
-
-
-def place_kernel(in_ref, out_ref, tile_ref):
-    low = low_lanes(128)
-    squares = jnp.zeros((8, 128), F32)
-    for row in range(N_ROW):
-        squares = squares + in_ref[row, 128:136, :].astype(F32)
-    squares = jnp.sum(squares, axis=0, keepdims=True)
+    last = total - high - middle
+    row = lax.broadcasted_iota(jnp.int32, (2, 128), 0)
+    lane = lax.broadcasted_iota(jnp.int32, (2, 128), 1)
+    rows = jnp.where(row == 0, high, jnp.where(lane < 64, middle, last))
+    for peer in range(N_ROW * N_X):
+        packed[34 * peer : 34 * peer + 32, :] = in_ref[peer].astype(F32)
+        packed[34 * peer + 32 : 34 * peer + 34, :] = rows
+    out_ref[...] = packed[...].astype(BF16)
+
+
+def place_kernel(in_ref, out_ref, packed, tile_ref):
+    packed[...] = in_ref[...].astype(F32)
+    squares = jnp.zeros((2, 128), F32)
+    for peer in range(N_ROW * N_X):
+        squares = squares + packed[34 * peer + 32 : 34 * peer + 34, :]
+    squares = squares[:1, :1] + squares[1:, :1] + squares[1:, 64:65]
     factor = jnp.minimum(1.0, jnp.sqrt(jnp.float32(FF * D)) / jnp.sqrt(squares + 1e-06))
 
-    def piece(row):
-        return in_ref[row, :128, :].astype(F32)
-
+    for s in range(4):
+        for j in range(8):
+            for half in range(2):
+                peers = [8 * j + 4 * a + 2 * half + q for a in range(2) for q in range(2)]
+                starts = [34 * peer + 8 * s for peer in peers]
+                tiles = [packed[start : start + 8, :] * factor for start in starts]
+                for r in range(4):
+                    start = (4 * s + r) * 8
+                    value = gather_group(tiles, r)
+                    if half == 0 and j == 7:
+                        value = value + tile_ref[7, start : start + 8, :]
+                    tile_ref[j + 7 * half, start : start + 8, :] = value
     for tile in range(15):
-        if tile < 7:
-            value = jnp.where(low, piece(2 * tile), swap_halves(piece(2 * tile + 1)))
-        elif tile == 7:
-            value = jnp.where(low, piece(14) + swap_halves(piece(0)), piece(1))
-        elif tile < 14:
-            value = jnp.where(
-                low, swap_halves(piece(2 * tile - 14)), piece(2 * tile - 13)
-            )
-        else:
-            value = swap_halves(piece(14))
-        tile_ref[...] = value * factor
         end = min(128 * tile + 128, WIDTH)
         for l in range(8):
-            rows = tile_ref[pl.ds(l, 16, stride=8), :]
+            rows = tile_ref[tile, pl.ds(l, 16, stride=8), :]
             out_ref[l, :, 128 * tile : end] = rows[:, : end - 128 * tile]
 
 
@@ -288,26 +309,32 @@
     packed = lax.all_to_all(packed, ROW_Z, 0, 0, tiled=True)
     spread = call(
         spread_kernel,
-        shape((N_X, 1088, 128), BF16),
+        shape((N_X, 512, 128), BF16),
         vmem(1),
         [pltpu.VMEM((N_ROW * N_Z * 10, 128), F32)],
     )(packed.reshape(N_ROW * N_Z * 10, 128))
     spread = lax.all_to_all(spread, "col_0", 0, 0, tiled=True)
+    peers = N_ROW * N_X
     mixed, squares = call(
         product_kernel,
-        (shape((N_ROW, 128, 128), BF16), shape((N_COL, 1, 128), F32)),
+        (shape((peers, 32, 128), BF16), shape((N_Z, 1, 128), F32)),
         vmem(2),
         [pltpu.VMEM((2048, 128), F32)],
     )(spread, mix)
-    squares = lax.all_to_all(squares, COL, 0, 0, tiled=True)
-    mixed = call(carry_kernel, shape((N_ROW, 136, 128), BF16), vmem(2))(mixed, squares)
-    mixed = lax.all_to_all(mixed, ROW, 0, 0, tiled=True)
+    squares = lax.all_to_all(squares, "col_1", 0, 0, tiled=True)
+    mixed = call(
+        carry_kernel,
+        shape((peers * 34, 128), BF16),
+        vmem(2),
+        [pltpu.VMEM((peers * 34, 128), F32)],
+    )(mixed, squares)
+    mixed = lax.all_to_all(mixed.reshape(peers, 17, 2, 128), ROW_X, 0, 0, tiled=True)
     return call(
         place_kernel,
         shape((8, 16, WIDTH), F32),
         vmem(1),
-        [pltpu.VMEM((128, 128), F32)],
-    )(mixed)
+        [pltpu.VMEM((peers * 34, 128), F32), pltpu.VMEM((15, 128, 128), F32)],
+    )(mixed.reshape(peers * 34, 128))
 
 
 def solution(mesh):

time: 95.8 us -> 87.8 us (0.916)
  waiting for transfers between devices: 15.2 us -> 8.27 us
  blocking collectives: 69.3 us -> 67.3 us
    all_to_all x1, waiting for transfers between devices: 15.2 us -> 8.27 us  [shards(): spread = lax.all_to_all(spread, 'col_0', 0, 0, tiled=True)]
    all_to_all x2, blocking collectives: 34.4 us -> 32.3 us  [the longest x1 23.4 us: shards(): lax.all_to_all(mixed.reshape(peers, 17, 2, 128), ROW_X, 0, 0, tiled=True)]
where the time goes in v3:
time: 87.8 us; the launch traced here: 87.4 us
  blocking collectives  67.3 us (77%)
  waiting for transfers between devices  8.27 us (9%)
  Pallas kernels  5.55 us (6%)
  starting transfers between devices  4.14 us (5%)
  local copies, waits for them, and re-layouts  2.11 us (2%)
    all_to_all x1, blocking collectives, shards(): packed = lax.all_to_all(packed, ROW_Z, 0, 0, tiled=True)  34.9 us
    all_to_all x1, blocking collectives, shards(): lax.all_to_all(mixed.reshape(peers, 17, 2, 128), ROW_X, 0, 0, tiled=True)  23.4 us
    all_to_all x1, blocking collectives, shards(): squares = lax.all_to_all(squares, 'col_1', 0, 0, tiled=True)  8.9 us
    all_to_all x1, waiting for transfers between devices, shards(): spread = lax.all_to_all(spread, 'col_0', 0, 0, tiled=True)  8.27 us
    all_to_all x1, starting transfers between devices, shards(): spread = lax.all_to_all(spread, 'col_0', 0, 0, tiled=True)  4.14 us
    unnamed x10, local copies, waits for them, and re-layouts  2.11 us
  transfers between devices with their start and end apart: 1, of which 1 were waited for; matrix products, arithmetic and copies ran while one was open for 0% of the time, Pallas kernels for 1%

profile of v3, /device:TPU:1, one launch (start us, length us, event | category | flops | bytes accessed | tf_op | source)
XLA Modules:
  0.0 87.4 jit_solution(8839591730324030183)
XLA Ops:
  0.0 0.0 copy-start
  0.0 0.8 copy-done
  0.8 0.0 copy-start.2
  0.8 0.7 copy-done.2
  1.4 0.3 shard_map.55
  1.7 34.9 %all_to_all.20 = bf16[128,5,2,128]{3,2,1,0:T(2,128)(2,1)S(1)} all-to-all(bf16[128,5,2,128]{3,2,1,0:T(2,128)(2,1)S(1)} %bitcast.9), channel_id=1, replica_groups=mesh['row_0'=8,'row_1'=2,'col_0'=4,'col_1'=8] {'row_0','row_1','col_1'}, dimensions={0} | all-to-all | bytes 655360 | tf_op jit(solution)/shard_map/all_to_all | solution.py:309
  36.7 1.1 %shard_map.56 = bf16[4,512,128]{2,1,0:T(8,128)(2,1)} custom-call(bf16[1280,128]{1,0:T(8,128)(2,1)S(1)} %bitcast.8), custom_call_target="tpu_custom_call" | custom-call | tf_op jit(solution)/shard_map/pallas_call | solution.py:310
  37.8 0.0 copy-start.1
  37.8 4.1 %all-to-all-start.1 = ((bf16[4,512,128]{2,1,0:T(8,128)(2,1)}), bf16[4,512,128]{2,1,0:T(8,128)(2,1)S(1)}, u32[]{:S(2)}, u32[]{:S(2)}) async-start(bf16[4,512,128]{2,1,0:T(8,128)(2,1)} %shard_map.56), calls=%async_computation.1 | async-start | bytes 1048576 | tf_op jit(solution)/shard_map/all_to_all | solution.py:316
  41.9 0.0 copy-start.3
  41.9 0.0 copy-start.4
  41.9 0.0 copy-done.1
  41.9 0.6 copy-done.3
  42.6 0.0 copy-done.4
  42.6 1.0 %shard_map.57.mix_ref = bf16[128,128]{1,0:T(8,128)(2,1)S(1)} custom-call(s32[1,32]{1,0:T(1,128)S(1)} %bitcast.10, s32[1,16]{1,0:T(1,128)S(1)} %bitcast.11, s32[16,32]{1,0:T(8,128)S(1)} %copy-done.1), custom_call_target="tpu_custom_call" | custom-call | tf_op jit(solution)/shard_map/pallas_call | solution.py:305
  43.6 8.3 %all-to-all-done.1.in_ref = bf16[4,512,128]{2,1,0:T(8,128)(2,1)S(1)} async-done(((bf16[4,512,128]{2,1,0:T(8,128)(2,1)}), bf16[4,512,128]{2,1,0:T(8,128)(2,1)S(1)}, u32[]{:S(2)}, u32[]{:S(2)}) %all-to-all-start.1) | async-done | bytes 524320 | tf_op jit(solution)/shard_map/all_to_all | solution.py:316
  51.9 1.5 %shard_map.58 = (bf16[64,32,128]{2,1,0:T(8,128)(2,1)S(1)}, f32[8,1,128]{2,1,0:T(1,128)S(1)}) custom-call(bf16[4,512,128]{2,1,0:T(8,128)(2,1)S(1)} %all-to-all-done.1.in_ref, bf16[128,128]{1,0:T(8,128)(2,1)S(1)} %shard_map.57.mix_ref), custom_call_target="tpu_custom_call" | custom-call | tf_op jit(solution)/shard_map/pallas_call | solution.py:318
  53.4 8.9 %all_to_all.21.squares_ref = f32[8,1,128]{2,1,0:T(1,128)S(1)} all-to-all(f32[8,1,128]{2,1,0:T(1,128)S(1)} %get-tuple-element.8), channel_id=1, replica_groups=mesh['row_0'=8,'row_1'=2,'col_0'=4,'col_1'=8] {'col_1'}, dimensions={0} | all-to-all | bytes 8192 | tf_op jit(solution)/shard_map/all_to_all | solution.py:324
  62.3 0.1 shard_map.59
  62.4 23.4 %all_to_all.22 = bf16[64,17,2,128]{3,2,1,0:T(2,128)(2,1)S(1)} all-to-all(bf16[64,17,2,128]{3,2,1,0:T(2,128)(2,1)S(1)} %bitcast.6), channel_id=1, replica_groups=mesh['row_0'=8,'row_1'=2,'col_0'=4,'col_1'=8] {'row_0','row_1','col_0'}, dimensions={0} | all-to-all | bytes 1114112 | tf_op jit(solution)/shard_map/all_to_all | solution.py:331
  85.8 1.5 %shard_map.60 = f32[8,16,1848]{2,1,0:T(8,128)} custom-call(bf16[2176,128]{1,0:T(8,128)(2,1)S(1)} %bitcast.7), custom_call_target="tpu_custom_call" | custom-call | tf_op jit(solution)/shard_map/pallas_call | solution.py:332
Async XLA Ops:
  0.0 0.8 copy-start
  0.8 0.7 copy-start.2
  37.8 4.2 %copy-start.1 = (s32[16,32]{1,0:T(8,128)S(1)}, s32[16,32]{1,0:T(8,128)}, u32[]{:S(2)}) copy-start(s32[16,32]{1,0:T(8,128)} %mask_ref.1) | copy-start | bytes 6148
  37.8 14.1 %all-to-all-start.1 = ((bf16[4,512,128]{2,1,0:T(8,128)(2,1)}), bf16[4,512,128]{2,1,0:T(8,128)(2,1)S(1)}, u32[]{:S(2)}, u32[]{:S(2)}) async-start(bf16[4,512,128]{2,1,0:T(8,128)(2,1)} %shard_map.56), calls=%async_computation.1 | async-start | bytes 1048576 | tf_op jit(solution)/shard_map/all_to_all | solution.py:316
  41.9 0.7 copy-start.3
  41.9 0.7 copy-start.4

commit v4 on v3

--- a/solution.py
+++ b/solution.py
@@ -12,8 +12,8 @@
 FF = 29568
 ROW = ("row_0", "row_1")
 COL = ("col_0", "col_1")
-ROW_X = ("row_0", "row_1", "col_0")
-ROW_Z = ("row_0", "row_1", "col_1")
+X_ROW = ("col_0", "row_1", "row_0")
+Z_ROW = ("col_1", "row_1", "row_0")
 N_ROW = 16
 N_X = 4
 N_Z = 8
@@ -27,6 +27,10 @@
 VMEM_LIMIT = 48 * 1024 * 1024
 
 
+def place_among(other, row):
+    return (other * 2 + row % 2) * (N_ROW // 2) + row // 2
+
+
 def low_lanes(rows):
     return lax.broadcasted_iota(jnp.int32, (rows, 128), 1) < 64
 
@@ -35,7 +39,26 @@
     return pltpu.roll(tile, 64, 1)
 
 
-def pack_kernel(acts_ref, errs_ref, out_ref, padded, packed):
+def pack_kernel(
+    acts_in, errs_in, cols_in, rows_in, mask_in,
+    out_ref, cols_ref, rows_ref, mask_ref,
+    acts_ref, errs_ref, padded, packed, sems,
+):
+    pairs = (
+        (acts_in, acts_ref),
+        (errs_in, errs_ref),
+        (cols_in, cols_ref),
+        (rows_in, rows_ref),
+        (mask_in, mask_ref),
+    )
+    copies = [
+        pltpu.make_async_copy(source, target, sems.at[i])
+        for i, (source, target) in enumerate(pairs)
+    ]
+    for copy in copies:
+        copy.start()
+    for copy in copies:
+        copy.wait()
     padded[...] = jnp.zeros_like(padded)
     padded[:, :HALF] = acts_ref[...].astype(F32)
     plain = padded[...]
@@ -55,7 +78,7 @@
         for v in range(1, 4):
             turned = pltpu.roll(both, 32 * v, 1)
             tile = jnp.where(quarter == v, turned[2 * v : 2 * v + 2], tile)
-        err_tiles.append(tile)
+        err_tiles.append(pltpu.roll(tile, 16 * lax.axis_index("row_0"), 1))
     for row in range(N_ROW):
         lanes = slice(128 * (row // 2), 128 * (row // 2) + 128)
         upper, lower = acts[:8, lanes], acts[8:, lanes]
@@ -65,29 +88,30 @@
             tile = jnp.where(low, swap_halves(upper), lower)
         tile = pltpu.roll(tile, up, 1)
         for z in range(N_Z):
-            start = (row * N_Z + z) * 10
+            start = place_among(z, row) * 10
             packed[start : start + 8, :] = tile
             packed[start + 8 : start + 10, :] = err_tiles[z]
-    out_ref[...] = packed[...].astype(BF16)
+    out_ref[...] = packed[: out_ref.shape[0], :].astype(BF16)
 
 
 def gather_group(tiles, which):
+    count = len(tiles)
+    width = 128 // count
     rows = tiles[0].shape[0]
-    wanted = lax.broadcasted_iota(jnp.int32, (rows, 128), 1) // 32
-    result = tiles[-which % 4]
-    for place in range(1, 4):
-        result = jnp.where(wanted == place, tiles[(place - which) % 4], result)
-    return pltpu.roll(result, 128 - 32 * which, 1) if which else result
+    wanted = lax.broadcasted_iota(jnp.int32, (rows, 128), 1) // width
+    result = tiles[-which % count]
+    for place in range(1, count):
+        result = jnp.where(wanted == place, tiles[(place - which) % count], result)
+    return pltpu.roll(result, 128 - width * which, 1) if which else result
 
 
 def spread_kernel(in_ref, out_ref, packed):
-    packed[...] = in_ref[...].astype(F32)
-    group = lax.broadcasted_iota(jnp.int32, (8, 128), 1) // 16
+    packed[: in_ref.shape[0], :] = in_ref[...].astype(F32)
     for pair in range(N_ROW // 2):
         for half in range(2):
             sources = []
             for row in (2 * pair, 2 * pair + 1):
-                starts = [(row * N_Z + z) * 10 for z in range(half, N_Z, 2)]
+                starts = [place_among(z, row) * 10 for z in range(half, N_Z, 2)]
                 sources.append([packed[s : s + 8, :] for s in starts])
             for part in range(2):
                 for q in range(2):
@@ -97,27 +121,22 @@
                     start = 128 * part + 16 * pair
                     out_ref[2 * half + q, start : start + 16, :] = both.astype(BF16)
     for parity in range(2):
-        sums = [[jnp.zeros((8, 128), F32) for _ in range(8)] for _ in range(2)]
-        for block in range(8):
-            for part in range(2):
+        pieces = [[], []]
+        for part in range(2):
+            sources = []
+            for block in range(8):
                 starts = [
-                    ((2 * block + parity) * N_Z + z) * 10 + 8
+                    place_among(z, 2 * block + parity) * 10 + 8
                     for z in range(part, N_Z, 2)
                 ]
-                source = jnp.concatenate(
-                    [packed[s : s + 2, :] for s in starts], axis=0
+                sources.append(
+                    jnp.concatenate([packed[s : s + 2, :] for s in starts], axis=0)
                 )
-                for v in range(4):
-                    for q in range(2):
-                        turned = pltpu.roll(
-                            source, (128 + 16 * (block - q) - 32 * v) % 128, 1
-                        )
-                        place = 4 * part + v
-                        sums[q][place] = jnp.where(
-                            group == block, turned, sums[q][place]
-                        )
+            for v in range(4):
+                for q in range(2):
+                    pieces[q].append(gather_group(sources, 2 * v + q))
         for q in range(2):
-            errs = jnp.concatenate(sums[q], axis=0).astype(BF16)
+            errs = jnp.concatenate(pieces[q], axis=0).astype(BF16)
             start = 256 + 64 * (2 * parity + q)
             for x in range(N_X):
                 out_ref[x, start : start + 64, :] = errs
@@ -131,7 +150,7 @@
     return (1 - 2 * (count % 2)).astype(F32)
 
 
-def mix_kernel(cols_ref, rows_ref, mask_ref, out_ref):
+def mix_matrix(cols_ref, rows_ref, mask_ref):
     iota = functools.partial(lax.broadcasted_iota, jnp.int32)
     cols = cols_ref[...]
     rows = rows_ref[...]
@@ -168,14 +187,13 @@
         decode = term / jnp.sum(term, axis=0, keepdims=True)
         left.append(decode * decode_errs[i : i + 1, :])
         right.append(encode_acts * encode_errs[i : i + 1, :])
-    total = lax.dot_general(
+    return lax.dot_general(
         jnp.concatenate(left, axis=0),
         jnp.concatenate(right, axis=0),
         (((0,), (0,)), ((), ())),
         preferred_element_type=F32,
         precision=lax.Precision.HIGHEST,
-    )
-    out_ref[...] = total.astype(BF16)
+    ).astype(BF16)
 
 
 def one_hot(source, size):
@@ -183,7 +201,10 @@
     return jnp.where(here == source, 1.0, 0.0).astype(BF16)
 
 
-def product_kernel(in_ref, mix_ref, out_ref, squares_ref, products):
+def product_kernel(
+    in_ref, cols_ref, rows_ref, mask_ref, out_ref, squares_ref, products
+):
+    mix = mix_matrix(cols_ref, rows_ref, mask_ref)
     to = lax.broadcasted_iota(jnp.int32, (256, 256), 1)
     tokens = one_hot(
         to // 32 * 32 + to // 2 % 4 * 8 + to // 8 % 4 * 2 + to % 2, 256
@@ -210,27 +231,32 @@
     errs = jnp.concatenate(
         [tile[32 * r : 32 * r + 32, :] for r in range(4) for tile in turned], axis=0
     )
-    for x in range(N_X):
-        product = jnp.dot(errs, in_ref[x, :256, :], preferred_element_type=F32)
-        tiles = [product[128 * r : 128 * r + 128, :] for r in range(4)]
-        tiles = [pltpu.roll(tile, 32 * r, 1) if r else tile for r, tile in enumerate(tiles)]
-        for i in range(4):
-            products[pl.ds(4 * x + i, 128, stride=16), :] = gather_group(tiles, i)
-    mix = mix_ref[...]
-    squares = jnp.zeros((128, 128), F32)
+    for x in range(0, N_X, 2):
+        acts = jnp.concatenate([in_ref[x, :256, :], in_ref[x + 1, :256, :]], axis=1)
+        product = jnp.dot(errs, acts, preferred_element_type=F32)
+        for i in range(2):
+            tiles = []
+            for r in range(4):
+                tile = product[128 * r : 128 * r + 128, 128 * i : 128 * i + 128]
+                tiles.append(pltpu.roll(tile, 32 * r, 1) if r else tile)
+            for z in range(4):
+                where = pl.ds(4 * (x + i) + z, 128, stride=16)
+                products[where, :] = gather_group(tiles, z)
+    squares = jnp.zeros((128, 256), F32)
     for pair in range(8):
-        mixed = []
-        for s in (2 * pair, 2 * pair + 1):
-            piece = products[128 * s : 128 * s + 128, :].astype(BF16)
-            grad = jnp.dot(mix, piece, preferred_element_type=F32)
-            squares = squares + grad * grad
-            mixed.append(grad)
+        both = [
+            products[128 * s : 128 * s + 128, :].astype(BF16)
+            for s in (2 * pair, 2 * pair + 1)
+        ]
+        grad = jnp.dot(mix, jnp.concatenate(both, axis=1), preferred_element_type=F32)
+        squares = squares + grad * grad
+        mixed = [grad[:, :128], grad[:, 128:]]
         start = 16 * (pair % 2)
         for k in range(N_ROW):
             both = jnp.concatenate(
                 [grad[8 * k : 8 * k + 8, :] for grad in mixed], axis=0
             )
-            out_ref[N_X * k + pair // 2, start : start + 16, :] = both.astype(BF16)
+            out_ref[place_among(pair // 2, k), start : start + 16, :] = both.astype(BF16)
     squares_ref[...] = jnp.full(squares_ref.shape, jnp.sum(squares), F32)
 
 
@@ -245,11 +271,11 @@
     for peer in range(N_ROW * N_X):
         packed[34 * peer : 34 * peer + 32, :] = in_ref[peer].astype(F32)
         packed[34 * peer + 32 : 34 * peer + 34, :] = rows
-    out_ref[...] = packed[...].astype(BF16)
+    out_ref[...] = packed[: out_ref.shape[0], :].astype(BF16)
 
 
 def place_kernel(in_ref, out_ref, packed, tile_ref):
-    packed[...] = in_ref[...].astype(F32)
+    packed[: in_ref.shape[0], :] = in_ref[...].astype(F32)
     squares = jnp.zeros((2, 128), F32)
     for peer in range(N_ROW * N_X):
         squares = squares + packed[34 * peer + 32 : 34 * peer + 34, :]
@@ -259,7 +285,9 @@
     for s in range(4):
         for j in range(8):
             for half in range(2):
-                peers = [8 * j + 4 * a + 2 * half + q for a in range(2) for q in range(2)]
+                peers = [
+                    place_among(2 * half + q, 2 * j + a) for a in range(2) for q in range(2)
+                ]
                 starts = [34 * peer + 8 * s for peer in peers]
                 tiles = [packed[start : start + 8, :] * factor for start in starts]
                 for r in range(4):
@@ -293,47 +321,55 @@
 
 def shards(hidden_acts, output_errors, col_points, row_points, worker_mask):
     shape = jax.ShapeDtypeStruct
-    packed = call(
+    args = (
+        hidden_acts,
+        output_errors,
+        col_points[None, :],
+        row_points[None, :],
+        worker_mask,
+    )
+    points = tuple(shape(arg.shape, arg.dtype) for arg in args[2:])
+    packed, *points = call(
         pack_kernel,
-        shape((N_ROW * N_Z * 10, 128), BF16),
-        vmem(2),
+        (shape((N_ROW * N_Z * 10, 128), BF16), *points),
+        [pl.BlockSpec(memory_space=pltpu.HBM)] * 5,
         [
+            pltpu.VMEM((16, HALF), BF16),
+            pltpu.VMEM((8, 256), BF16),
             pltpu.VMEM((16, 1024), F32),
-            pltpu.VMEM((N_ROW * N_Z * 10, 128), F32),
+            pltpu.VMEM((N_ROW * N_Z * 10 + 8, 128), F32),
+            pltpu.SemaphoreType.DMA((5,)),
         ],
-    )(hidden_acts, output_errors)
-    mix = call(mix_kernel, shape((128, 128), BF16), vmem(3))(
-        col_points[None, :], row_points[None, :], worker_mask
-    )
+    )(*[pltpu.with_memory_space_constraint(arg, pltpu.HBM) for arg in args])
     packed = packed.reshape(N_ROW * N_Z, 5, 2, 128)
-    packed = lax.all_to_all(packed, ROW_Z, 0, 0, tiled=True)
+    packed = lax.all_to_all(packed, Z_ROW, 0, 0, tiled=True)
     spread = call(
         spread_kernel,
         shape((N_X, 512, 128), BF16),
         vmem(1),
-        [pltpu.VMEM((N_ROW * N_Z * 10, 128), F32)],
+        [pltpu.VMEM((N_ROW * N_Z * 10 + 8, 128), F32)],
     )(packed.reshape(N_ROW * N_Z * 10, 128))
     spread = lax.all_to_all(spread, "col_0", 0, 0, tiled=True)
     peers = N_ROW * N_X
     mixed, squares = call(
         product_kernel,
         (shape((peers, 32, 128), BF16), shape((N_Z, 1, 128), F32)),
-        vmem(2),
-        [pltpu.VMEM((2048, 128), F32)],
-    )(spread, mix)
+        vmem(4),
+        [pltpu.VMEM((2048 + 16, 128), F32)],
+    )(spread, *points)
     squares = lax.all_to_all(squares, "col_1", 0, 0, tiled=True)
     mixed = call(
         carry_kernel,
         shape((peers * 34, 128), BF16),
         vmem(2),
-        [pltpu.VMEM((peers * 34, 128), F32)],
+        [pltpu.VMEM((peers * 34 + 8, 128), F32)],
     )(mixed, squares)
-    mixed = lax.all_to_all(mixed.reshape(peers, 17, 2, 128), ROW_X, 0, 0, tiled=True)
+    mixed = lax.all_to_all(mixed.reshape(peers, 17, 2, 128), X_ROW, 0, 0, tiled=True)
     return call(
         place_kernel,
         shape((8, 16, WIDTH), F32),
         vmem(1),
-        [pltpu.VMEM((peers * 34, 128), F32), pltpu.VMEM((15, 128, 128), F32)],
+        [pltpu.VMEM((peers * 34 + 8, 128), F32), pltpu.VMEM((15, 128 + 8, 128), F32)],
     )(mixed.reshape(peers * 34, 128))
 
 

time: 87.8 us -> 86.7 us (0.987)
  blocking collectives: 67.3 us -> 81 us
  waiting for transfers between devices: 8.27 us -> 0 us
  starting transfers between devices: 4.14 us -> 0 us
  local copies, waits for them, and re-layouts: 2.11 us -> 0 us
    all_to_all x2 -> x3, blocking collectives: 58.4 us -> 70.8 us  [the longest x1 34 us: shards(): packed = lax.all_to_all(packed, Z_ROW, 0, 0, tiled=True)]
    all_to_all x1 -> x0, waiting for transfers between devices: 8.27 us -> none  [shards(): spread = lax.all_to_all(spread, 'col_0', 0, 0, tiled=True)]
    all_to_all x1 -> x0, starting transfers between devices: 4.14 us -> none  [shards(): spread = lax.all_to_all(spread, 'col_0', 0, 0, tiled=True)]
    unnamed x10 -> x0, local copies, waits for them, and re-layouts: 2.11 us -> none
    all_to_all x1, blocking collectives: 8.9 us -> 10.2 us  [shards(): squares = lax.all_to_all(squares, 'col_1', 0, 0, tiled=True)]
  transfers between devices with their start and end apart: 1 -> 0, of which waited for: 1 -> 0; matrix products, arithmetic and copies ran while one was open for 0% -> 0% of each run, Pallas kernels for 1% -> 0%
where the time goes in v4:
time: 86.7 us; the launch traced here: 86.4 us
  blocking collectives  81 us (93%)
  Pallas kernels  5.35 us (6%)
    all_to_all x1, blocking collectives, shards(): packed = lax.all_to_all(packed, Z_ROW, 0, 0, tiled=True)  34 us
    all_to_all x1, blocking collectives, shards(): lax.all_to_all(mixed.reshape(peers, 17, 2, 128), X_ROW, 0, 0, tiled=True)  24.6 us
    all_to_all x1, blocking collectives, shards(): spread = lax.all_to_all(spread, 'col_0', 0, 0, tiled=True)  12.3 us
    all_to_all x1, blocking collectives, shards(): squares = lax.all_to_all(squares, 'col_1', 0, 0, tiled=True)  10.2 us
    pallas_call x1, Pallas kernels, shards(): call(product_kernel, (shape((peers, 32, 128), BF16), shape((N_Z, 1, 128),...  2.33 us

profile of v4, /device:TPU:1, one launch (start us, length us, event | category | flops | bytes accessed | tf_op | source)
XLA Modules:
  0.0 86.4 jit_solution(15342282214197108145)
XLA Ops:
  0.0 1.1 %shard_map.55 = (bf16[1280,128]{1,0:T(8,128)(2,1)S(1)}, s32[1,32]{1,0:T(1,128)S(1)}, s32[1,16]{1,0:T(1,128)S(1)}, s32[16,32]{1,0:T(8,128)S(1)}) custom-call(bf16[16,924]{1,0:T(8,128)(2,1)} %acts_in.1, bf16[8,256]{1,0:T(8,128)(2,1)} %errs_in.1, s32[1,32]{1,0:T(1,128)} %bitcast.10, s32[1,16]{1,0:T(1,128)} %bitcast.11, s32[16,32]{1,0:T(8,128)} %mask_in.1), custom_call_target="tpu_custom_call" | custom-call | tf_op jit(solution)/shard_map/pallas_call | solution.py:332
  1.1 34.0 %all_to_all.20 = bf16[128,5,2,128]{3,2,1,0:T(2,128)(2,1)S(1)} all-to-all(bf16[128,5,2,128]{3,2,1,0:T(2,128)(2,1)S(1)} %bitcast.9), channel_id=1, replica_groups=mesh['row_0'=8,'row_1'=2,'col_0'=4,'col_1'=8] {'col_1','row_1','row_0'}, dimensions={0} | all-to-all | bytes 655360 | tf_op jit(solution)/shard_map/all_to_all | solution.py:345
  35.1 0.2 shard_map.56
  35.4 12.3 %all_to_all.21.in_ref = bf16[4,512,128]{2,1,0:T(8,128)(2,1)S(1)} all-to-all(bf16[4,512,128]{2,1,0:T(8,128)(2,1)S(1)} %shard_map.56), channel_id=1, replica_groups=mesh['row_0'=8,'row_1'=2,'col_0'=4,'col_1'=8] {'col_0'}, dimensions={0} | all-to-all | bytes 1048576 | tf_op jit(solution)/shard_map/all_to_all | solution.py:352
  47.7 2.3 %shard_map.57 = (bf16[64,32,128]{2,1,0:T(8,128)(2,1)S(1)}, f32[8,1,128]{2,1,0:T(1,128)S(1)}) custom-call(bf16[4,512,128]{2,1,0:T(8,128)(2,1)S(1)} %all_to_all.21.in_ref, s32[1,32]{1,0:T(1,128)S(1)} %get-tuple-element.12.cols_ref, s32[1,16]{1,0:T(1,128)S(1)} %get-tuple-element.13.rows_ref, s32[16,32]{1,0:T(8,128)S(1)} %get-tuple-element.14.mask_ref), custom_call_target="tpu_custom_call" | custom-call | tf_op jit(solution)/shard_map/pallas_call | solution.py:354
  50.0 10.2 %all_to_all.22.squares_ref = f32[8,1,128]{2,1,0:T(1,128)S(1)} all-to-all(f32[8,1,128]{2,1,0:T(1,128)S(1)} %get-tuple-element.16), channel_id=1, replica_groups=mesh['row_0'=8,'row_1'=2,'col_0'=4,'col_1'=8] {'col_1'}, dimensions={0} | all-to-all | bytes 8192 | tf_op jit(solution)/shard_map/all_to_all | solution.py:360
  60.2 0.1 shard_map.58
  60.3 24.6 %all_to_all.23 = bf16[64,17,2,128]{3,2,1,0:T(2,128)(2,1)S(1)} all-to-all(bf16[64,17,2,128]{3,2,1,0:T(2,128)(2,1)S(1)} %bitcast.6), channel_id=1, replica_groups=mesh['row_0'=8,'row_1'=2,'col_0'=4,'col_1'=8] {'col_0','row_1','row_0'}, dimensions={0} | all-to-all | bytes 1114112 | tf_op jit(solution)/shard_map/all_to_all | solution.py:367
  84.8 1.5 %shard_map.59 = f32[8,16,1848]{2,1,0:T(8,128)} custom-call(bf16[2176,128]{1,0:T(8,128)(2,1)S(1)} %bitcast.7), custom_call_target="tpu_custom_call" | custom-call | tf_op jit(solution)/shard_map/pallas_call | solution.py:368

commit v5 on v4

--- a/solution.py
+++ b/solution.py
@@ -204,7 +204,6 @@
 def product_kernel(
     in_ref, cols_ref, rows_ref, mask_ref, out_ref, squares_ref, products
 ):
-    mix = mix_matrix(cols_ref, rows_ref, mask_ref)
     to = lax.broadcasted_iota(jnp.int32, (256, 256), 1)
     tokens = one_hot(
         to // 32 * 32 + to // 2 % 4 * 8 + to // 8 % 4 * 2 + to % 2, 256
@@ -242,6 +241,7 @@
             for z in range(4):
                 where = pl.ds(4 * (x + i) + z, 128, stride=16)
                 products[where, :] = gather_group(tiles, z)
+    mix = mix_matrix(cols_ref, rows_ref, mask_ref)
     squares = jnp.zeros((128, 256), F32)
     for pair in range(8):
         both = [
@@ -274,7 +274,7 @@
     out_ref[...] = packed[: out_ref.shape[0], :].astype(BF16)
 
 
-def place_kernel(in_ref, out_ref, packed, tile_ref):
+def place_kernel(in_ref, out_ref, packed, tile_ref, first_ref, second_ref, sems):
     packed[: in_ref.shape[0], :] = in_ref[...].astype(F32)
     squares = jnp.zeros((2, 128), F32)
     for peer in range(N_ROW * N_X):
@@ -282,38 +282,47 @@
     squares = squares[:1, :1] + squares[1:, :1] + squares[1:, 64:65]
     factor = jnp.minimum(1.0, jnp.sqrt(jnp.float32(FF * D)) / jnp.sqrt(squares + 1e-06))
 
-    for s in range(4):
-        for j in range(8):
-            for half in range(2):
-                peers = [
-                    place_among(2 * half + q, 2 * j + a) for a in range(2) for q in range(2)
-                ]
-                starts = [34 * peer + 8 * s for peer in peers]
-                tiles = [packed[start : start + 8, :] * factor for start in starts]
-                for r in range(4):
-                    start = (4 * s + r) * 8
-                    value = gather_group(tiles, r)
-                    if half == 0 and j == 7:
-                        value = value + tile_ref[7, start : start + 8, :]
-                    tile_ref[j + 7 * half, start : start + 8, :] = value
-    for tile in range(15):
-        end = min(128 * tile + 128, WIDTH)
-        for l in range(8):
-            rows = tile_ref[tile, pl.ds(l, 16, stride=8), :]
-            out_ref[l, :, 128 * tile : end] = rows[:, : end - 128 * tile]
+    copies = []
+    for part, staged in enumerate((first_ref, second_ref)):
+        for s in (2 * part, 2 * part + 1):
+            for j in range(8):
+                for half in range(2):
+                    peers = [
+                        place_among(2 * half + q, 2 * j + a) for a in range(2) for q in range(2)
+                    ]
+                    starts = [34 * peer + 8 * s for peer in peers]
+                    tiles = [packed[start : start + 8, :] * factor for start in starts]
+                    for r in range(4):
+                        start = (4 * s + r) * 8
+                        value = gather_group(tiles, r)
+                        if half == 0 and j == 7:
+                            value = value + tile_ref[7, start : start + 8, :]
+                        tile_ref[j + 7 * half, start : start + 8, :] = value
+        for tile in range(15):
+            end = min(128 * tile + 128, WIDTH)
+            for l in range(8):
+                rows = tile_ref[tile, pl.ds(64 * part + l, 8, stride=8), :]
+                staged[l, :, 128 * tile : end] = rows[:, : end - 128 * tile]
+        copy = pltpu.make_async_copy(
+            staged, out_ref.at[:, 8 * part : 8 * part + 8, :], sems.at[part]
+        )
+        copy.start()
+        copies.append(copy)
+    for copy in copies:
+        copy.wait()
 
 
 def vmem(count):
     return [pl.BlockSpec(memory_space=pltpu.VMEM) for _ in range(count)]
 
 
-def call(kernel, out, in_specs, scratch=()):
+def call(kernel, out, in_specs, scratch=(), out_space=pltpu.VMEM):
     many = isinstance(out, tuple)
     return pl.pallas_call(
         kernel,
         out_shape=out,
         in_specs=in_specs,
-        out_specs=tuple(vmem(len(out))) if many else vmem(1)[0],
+        out_specs=tuple(vmem(len(out))) if many else pl.BlockSpec(memory_space=out_space),
         scratch_shapes=list(scratch),
         compiler_params=pltpu.CompilerParams(vmem_limit_bytes=VMEM_LIMIT),
     )
@@ -369,7 +378,14 @@
         place_kernel,
         shape((8, 16, WIDTH), F32),
         vmem(1),
-        [pltpu.VMEM((peers * 34 + 8, 128), F32), pltpu.VMEM((15, 128 + 8, 128), F32)],
+        [
+            pltpu.VMEM((peers * 34 + 8, 128), F32),
+            pltpu.VMEM((15, 128 + 8, 128), F32),
+            pltpu.VMEM((8, 8, WIDTH), F32),
+            pltpu.VMEM((8, 8, WIDTH), F32),
+            pltpu.SemaphoreType.DMA((2,)),
+        ],
+        pltpu.HBM,
     )(mixed.reshape(peers * 34, 128))
 
 

time: 86.7 us -> 86.1 us (level)
  no operation moved by 1% of the time
where the time goes in v5:
time: 86.1 us; the launch traced here: 85.8 us
  blocking collectives  81 us (94%)
  Pallas kernels  4.77 us (6%)
    all_to_all x1, blocking collectives, shards(): packed = lax.all_to_all(packed, Z_ROW, 0, 0, tiled=True)  34 us
    all_to_all x1, blocking collectives, shards(): lax.all_to_all(mixed.reshape(peers, 17, 2, 128), X_ROW, 0, 0, tiled=True)  24.6 us
    all_to_all x1, blocking collectives, shards(): spread = lax.all_to_all(spread, 'col_0', 0, 0, tiled=True)  12.3 us
    all_to_all x1, blocking collectives, shards(): squares = lax.all_to_all(squares, 'col_1', 0, 0, tiled=True)  10.1 us
    pallas_call x1, Pallas kernels, shards(): call(product_kernel, (shape((peers, 32, 128), BF16), shape((N_Z, 1, 128),...  1.85 us

profile of v5, /device:TPU:1, one launch (start us, length us, event | category | flops | bytes accessed | tf_op | source)
XLA Modules:
  0.0 85.8 jit_solution(7967142342165583127)
XLA Ops:
  0.0 1.1 %shard_map.55 = (bf16[1280,128]{1,0:T(8,128)(2,1)S(1)}, s32[1,32]{1,0:T(1,128)S(1)}, s32[1,16]{1,0:T(1,128)S(1)}, s32[16,32]{1,0:T(8,128)S(1)}) custom-call(bf16[16,924]{1,0:T(8,128)(2,1)} %acts_in.1, bf16[8,256]{1,0:T(8,128)(2,1)} %errs_in.1, s32[1,32]{1,0:T(1,128)} %bitcast.10, s32[1,16]{1,0:T(1,128)} %bitcast.11, s32[16,32]{1,0:T(8,128)} %mask_in.1), custom_call_target="tpu_custom_call" | custom-call | tf_op jit(solution)/shard_map/pallas_call | solution.py:341
  1.1 34.0 %all_to_all.20 = bf16[128,5,2,128]{3,2,1,0:T(2,128)(2,1)S(1)} all-to-all(bf16[128,5,2,128]{3,2,1,0:T(2,128)(2,1)S(1)} %bitcast.9), channel_id=1, replica_groups=mesh['row_0'=8,'row_1'=2,'col_0'=4,'col_1'=8] {'col_1','row_1','row_0'}, dimensions={0} | all-to-all | bytes 655360 | tf_op jit(solution)/shard_map/all_to_all | solution.py:354
  35.1 0.2 shard_map.56
  35.4 12.3 %all_to_all.21.in_ref = bf16[4,512,128]{2,1,0:T(8,128)(2,1)S(1)} all-to-all(bf16[4,512,128]{2,1,0:T(8,128)(2,1)S(1)} %shard_map.56), channel_id=1, replica_groups=mesh['row_0'=8,'row_1'=2,'col_0'=4,'col_1'=8] {'col_0'}, dimensions={0} | all-to-all | bytes 1048576 | tf_op jit(solution)/shard_map/all_to_all | solution.py:361
  47.7 1.8 %shard_map.57 = (bf16[64,32,128]{2,1,0:T(8,128)(2,1)S(1)}, f32[8,1,128]{2,1,0:T(1,128)S(1)}) custom-call(bf16[4,512,128]{2,1,0:T(8,128)(2,1)S(1)} %all_to_all.21.in_ref, s32[1,32]{1,0:T(1,128)S(1)} %get-tuple-element.12.cols_ref, s32[1,16]{1,0:T(1,128)S(1)} %get-tuple-element.13.rows_ref, s32[16,32]{1,0:T(8,128)S(1)} %get-tuple-element.14.mask_ref), custom_call_target="tpu_custom_call" | custom-call | tf_op jit(solution)/shard_map/pallas_call | solution.py:363
  49.5 10.1 %all_to_all.22.squares_ref = f32[8,1,128]{2,1,0:T(1,128)S(1)} all-to-all(f32[8,1,128]{2,1,0:T(1,128)S(1)} %get-tuple-element.16), channel_id=1, replica_groups=mesh['row_0'=8,'row_1'=2,'col_0'=4,'col_1'=8] {'col_1'}, dimensions={0} | all-to-all | bytes 8192 | tf_op jit(solution)/shard_map/all_to_all | solution.py:369
  59.7 0.1 shard_map.58
  59.8 24.6 %all_to_all.23 = bf16[64,17,2,128]{3,2,1,0:T(2,128)(2,1)S(1)} all-to-all(bf16[64,17,2,128]{3,2,1,0:T(2,128)(2,1)S(1)} %bitcast.6), channel_id=1, replica_groups=mesh['row_0'=8,'row_1'=2,'col_0'=4,'col_1'=8] {'col_0','row_1','row_0'}, dimensions={0} | all-to-all | bytes 1114112 | tf_op jit(solution)/shard_map/all_to_all | solution.py:376
  84.4 1.4 %shard_map.59 = f32[8,16,1848]{2,1,0:T(8,128)} custom-call(bf16[2176,128]{1,0:T(8,128)(2,1)S(1)} %bitcast.7), custom_call_target="tpu_custom_call" | custom-call | tf_op jit(solution)/shard_map/pallas_call | solution.py:377

commit v6 on v5

--- a/solution.py
+++ b/solution.py
@@ -94,15 +94,22 @@
     out_ref[...] = packed[: out_ref.shape[0], :].astype(BF16)
 
 
-def gather_group(tiles, which):
+def gather_groups(tiles):
     count = len(tiles)
     width = 128 // count
     rows = tiles[0].shape[0]
-    wanted = lax.broadcasted_iota(jnp.int32, (rows, 128), 1) // width
-    result = tiles[-which % count]
-    for place in range(1, count):
-        result = jnp.where(wanted == place, tiles[(place - which) % count], result)
-    return pltpu.roll(result, 128 - width * which, 1) if which else result
+    group = lax.broadcasted_iota(jnp.int32, (rows, 128), 1) // width
+    step = 1
+    while step < count:
+        later = group // step % 2 == 1
+        tiles = [
+            jnp.where(later, tiles[(i + step) % count], tiles[i]) for i in range(count)
+        ]
+        step *= 2
+    results = [tiles[0]]
+    for which in range(1, count):
+        results.append(pltpu.roll(tiles[count - which], 128 - width * which, 1))
+    return results
 
 
 def spread_kernel(in_ref, out_ref, packed):
@@ -112,11 +119,11 @@
             sources = []
             for row in (2 * pair, 2 * pair + 1):
                 starts = [place_among(z, row) * 10 for z in range(half, N_Z, 2)]
-                sources.append([packed[s : s + 8, :] for s in starts])
+                sources.append(gather_groups([packed[s : s + 8, :] for s in starts]))
             for part in range(2):
                 for q in range(2):
                     both = jnp.concatenate(
-                        [gather_group(tiles, 2 * part + q) for tiles in sources], axis=0
+                        [tiles[2 * part + q] for tiles in sources], axis=0
                     )
                     start = 128 * part + 16 * pair
                     out_ref[2 * half + q, start : start + 16, :] = both.astype(BF16)
@@ -132,9 +139,9 @@
                 sources.append(
                     jnp.concatenate([packed[s : s + 2, :] for s in starts], axis=0)
                 )
-            for v in range(4):
-                for q in range(2):
-                    pieces[q].append(gather_group(sources, 2 * v + q))
+            gathered = gather_groups(sources)
+            for q in range(2):
+                pieces[q] += gathered[q::2]
         for q in range(2):
             errs = jnp.concatenate(pieces[q], axis=0).astype(BF16)
             start = 256 + 64 * (2 * parity + q)
@@ -238,10 +245,10 @@
             for r in range(4):
                 tile = product[128 * r : 128 * r + 128, 128 * i : 128 * i + 128]
                 tiles.append(pltpu.roll(tile, 32 * r, 1) if r else tile)
-            for z in range(4):
-                where = pl.ds(4 * (x + i) + z, 128, stride=16)
-                products[where, :] = gather_group(tiles, z)
-    mix = mix_matrix(cols_ref, rows_ref, mask_ref)
+            for z, tile in enumerate(gather_groups(tiles)):
+                products[pl.ds(4 * (x + i) + z, 128, stride=16), :] = tile
+        if x == 0:
+            mix = mix_matrix(cols_ref, rows_ref, mask_ref)
     squares = jnp.zeros((128, 256), F32)
     for pair in range(8):
         both = [
@@ -292,9 +299,8 @@
                     ]
                     starts = [34 * peer + 8 * s for peer in peers]
                     tiles = [packed[start : start + 8, :] * factor for start in starts]
-                    for r in range(4):
+                    for r, value in enumerate(gather_groups(tiles)):
                         start = (4 * s + r) * 8
-                        value = gather_group(tiles, r)
                         if half == 0 and j == 7:
                             value = value + tile_ref[7, start : start + 8, :]
                         tile_ref[j + 7 * half, start : start + 8, :] = value

time: 86.1 us -> 86 us (level)
  no operation moved by 1% of the time
where the time goes in v6:
time: 86 us; the launch traced here: 85.7 us
  blocking collectives  81 us (94%)
  Pallas kernels  4.71 us (5%)
    all_to_all x1, blocking collectives, shards(): packed = lax.all_to_all(packed, Z_ROW, 0, 0, tiled=True)  34 us
    all_to_all x1, blocking collectives, shards(): lax.all_to_all(mixed.reshape(peers, 17, 2, 128), X_ROW, 0, 0, tiled=True)  24.6 us
    all_to_all x1, blocking collectives, shards(): spread = lax.all_to_all(spread, 'col_0', 0, 0, tiled=True)  12.3 us
    all_to_all x1, blocking collectives, shards(): squares = lax.all_to_all(squares, 'col_1', 0, 0, tiled=True)  10.1 us
    pallas_call x1, Pallas kernels, shards(): call(product_kernel, (shape((peers, 32, 128), BF16), shape((N_Z, 1, 128),...  1.82 us

profile of v6, /device:TPU:1, one launch (start us, length us, event | category | flops | bytes accessed | tf_op | source)
XLA Modules:
  0.0 85.7 jit_solution(3640115473178272192)
XLA Ops:
  0.0 1.1 %shard_map.55 = (bf16[1280,128]{1,0:T(8,128)(2,1)S(1)}, s32[1,32]{1,0:T(1,128)S(1)}, s32[1,16]{1,0:T(1,128)S(1)}, s32[16,32]{1,0:T(8,128)S(1)}) custom-call(bf16[16,924]{1,0:T(8,128)(2,1)} %acts_in.1, bf16[8,256]{1,0:T(8,128)(2,1)} %errs_in.1, s32[1,32]{1,0:T(1,128)} %bitcast.10, s32[1,16]{1,0:T(1,128)} %bitcast.11, s32[16,32]{1,0:T(8,128)} %mask_in.1), custom_call_target="tpu_custom_call" | custom-call | tf_op jit(solution)/shard_map/pallas_call | solution.py:347
  1.1 34.0 %all_to_all.20 = bf16[128,5,2,128]{3,2,1,0:T(2,128)(2,1)S(1)} all-to-all(bf16[128,5,2,128]{3,2,1,0:T(2,128)(2,1)S(1)} %bitcast.9), channel_id=1, replica_groups=mesh['row_0'=8,'row_1'=2,'col_0'=4,'col_1'=8] {'col_1','row_1','row_0'}, dimensions={0} | all-to-all | bytes 655360 | tf_op jit(solution)/shard_map/all_to_all | solution.py:360
  35.1 0.2 shard_map.56
  35.3 12.3 %all_to_all.21.in_ref = bf16[4,512,128]{2,1,0:T(8,128)(2,1)S(1)} all-to-all(bf16[4,512,128]{2,1,0:T(8,128)(2,1)S(1)} %shard_map.56), channel_id=1, replica_groups=mesh['row_0'=8,'row_1'=2,'col_0'=4,'col_1'=8] {'col_0'}, dimensions={0} | all-to-all | bytes 1048576 | tf_op jit(solution)/shard_map/all_to_all | solution.py:367
  47.6 1.8 %shard_map.57 = (bf16[64,32,128]{2,1,0:T(8,128)(2,1)S(1)}, f32[8,1,128]{2,1,0:T(1,128)S(1)}) custom-call(bf16[4,512,128]{2,1,0:T(8,128)(2,1)S(1)} %all_to_all.21.in_ref, s32[1,32]{1,0:T(1,128)S(1)} %get-tuple-element.12.cols_ref, s32[1,16]{1,0:T(1,128)S(1)} %get-tuple-element.13.rows_ref, s32[16,32]{1,0:T(8,128)S(1)} %get-tuple-element.14.mask_ref), custom_call_target="tpu_custom_call" | custom-call | tf_op jit(solution)/shard_map/pallas_call | solution.py:369
  49.5 10.1 %all_to_all.22.squares_ref = f32[8,1,128]{2,1,0:T(1,128)S(1)} all-to-all(f32[8,1,128]{2,1,0:T(1,128)S(1)} %get-tuple-element.16), channel_id=1, replica_groups=mesh['row_0'=8,'row_1'=2,'col_0'=4,'col_1'=8] {'col_1'}, dimensions={0} | all-to-all | bytes 8192 | tf_op jit(solution)/shard_map/all_to_all | solution.py:375
  59.6 0.1 shard_map.58
  59.7 24.6 %all_to_all.23 = bf16[64,17,2,128]{3,2,1,0:T(2,128)(2,1)S(1)} all-to-all(bf16[64,17,2,128]{3,2,1,0:T(2,128)(2,1)S(1)} %bitcast.6), channel_id=1, replica_groups=mesh['row_0'=8,'row_1'=2,'col_0'=4,'col_1'=8] {'col_0','row_1','row_0'}, dimensions={0} | all-to-all | bytes 1114112 | tf_op jit(solution)/shard_map/all_to_all | solution.py:382
  84.3 1.4 %shard_map.59 = f32[8,16,1848]{2,1,0:T(8,128)} custom-call(bf16[2176,128]{1,0:T(8,128)(2,1)S(1)} %bitcast.7), custom_call_target="tpu_custom_call" | custom-call | tf_op jit(solution)/shard_map/pallas_call | solution.py:383

commit v7 on v6

--- a/solution.py
+++ b/solution.py
@@ -194,13 +194,20 @@
         decode = term / jnp.sum(term, axis=0, keepdims=True)
         left.append(decode * decode_errs[i : i + 1, :])
         right.append(encode_acts * encode_errs[i : i + 1, :])
-    return lax.dot_general(
-        jnp.concatenate(left, axis=0),
-        jnp.concatenate(right, axis=0),
+    left, right = jnp.concatenate(left, axis=0), jnp.concatenate(right, axis=0)
+    left_high, right_high = left.astype(BF16), right.astype(BF16)
+    left_low = (left - left_high.astype(F32)).astype(BF16)
+    right_low = (right - right_high.astype(F32)).astype(BF16)
+    both = lax.dot_general(
+        left_high,
+        jnp.concatenate([right_high, right_low], axis=1),
         (((0,), (0,)), ((), ())),
         preferred_element_type=F32,
-        precision=lax.Precision.HIGHEST,
-    ).astype(BF16)
+    )
+    rest = lax.dot_general(
+        left_low, right_high, (((0,), (0,)), ((), ())), preferred_element_type=F32
+    )
+    return (both[:, :128] + (both[:, 128:] + rest)).astype(BF16)
 
 
 def one_hot(source, size):

time: 86 us -> 85.9 us (level)
  no operation moved by 1% of the time
where the time goes in v7:
time: 85.9 us; the launch traced here: 85.6 us
  blocking collectives  81 us (94%)
  Pallas kernels  4.6 us (5%)
    all_to_all x1, blocking collectives, shards(): packed = lax.all_to_all(packed, Z_ROW, 0, 0, tiled=True)  34 us
    all_to_all x1, blocking collectives, shards(): lax.all_to_all(mixed.reshape(peers, 17, 2, 128), X_ROW, 0, 0, tiled=True)  24.6 us
    all_to_all x1, blocking collectives, shards(): spread = lax.all_to_all(spread, 'col_0', 0, 0, tiled=True)  12.3 us
    all_to_all x1, blocking collectives, shards(): squares = lax.all_to_all(squares, 'col_1', 0, 0, tiled=True)  10.1 us

profile of v7, /device:TPU:1, one launch (start us, length us, event | category | flops | bytes accessed | tf_op | source)
XLA Modules:
  0.0 85.6 jit_solution(10088089113985144108)
XLA Ops:
  0.0 1.1 %shard_map.55 = (bf16[1280,128]{1,0:T(8,128)(2,1)S(1)}, s32[1,32]{1,0:T(1,128)S(1)}, s32[1,16]{1,0:T(1,128)S(1)}, s32[16,32]{1,0:T(8,128)S(1)}) custom-call(bf16[16,924]{1,0:T(8,128)(2,1)} %acts_in.1, bf16[8,256]{1,0:T(8,128)(2,1)} %errs_in.1, s32[1,32]{1,0:T(1,128)} %bitcast.10, s32[1,16]{1,0:T(1,128)} %bitcast.11, s32[16,32]{1,0:T(8,128)} %mask_in.1), custom_call_target="tpu_custom_call" | custom-call | tf_op jit(solution)/shard_map/pallas_call | solution.py:354
  1.1 34.0 %all_to_all.20 = bf16[128,5,2,128]{3,2,1,0:T(2,128)(2,1)S(1)} all-to-all(bf16[128,5,2,128]{3,2,1,0:T(2,128)(2,1)S(1)} %bitcast.9), channel_id=1, replica_groups=mesh['row_0'=8,'row_1'=2,'col_0'=4,'col_1'=8] {'col_1','row_1','row_0'}, dimensions={0} | all-to-all | bytes 655360 | tf_op jit(solution)/shard_map/all_to_all | solution.py:367
  35.1 0.2 shard_map.56
  35.3 12.3 %all_to_all.21.in_ref = bf16[4,512,128]{2,1,0:T(8,128)(2,1)S(1)} all-to-all(bf16[4,512,128]{2,1,0:T(8,128)(2,1)S(1)} %shard_map.56), channel_id=1, replica_groups=mesh['row_0'=8,'row_1'=2,'col_0'=4,'col_1'=8] {'col_0'}, dimensions={0} | all-to-all | bytes 1048576 | tf_op jit(solution)/shard_map/all_to_all | solution.py:374
  47.6 1.7 %shard_map.57 = (bf16[64,32,128]{2,1,0:T(8,128)(2,1)S(1)}, f32[8,1,128]{2,1,0:T(1,128)S(1)}) custom-call(bf16[4,512,128]{2,1,0:T(8,128)(2,1)S(1)} %all_to_all.21.in_ref, s32[1,32]{1,0:T(1,128)S(1)} %get-tuple-element.12.cols_ref, s32[1,16]{1,0:T(1,128)S(1)} %get-tuple-element.13.rows_ref, s32[16,32]{1,0:T(8,128)S(1)} %get-tuple-element.14.mask_ref), custom_call_target="tpu_custom_call" | custom-call | tf_op jit(solution)/shard_map/pallas_call | solution.py:376
  49.4 10.1 %all_to_all.22.squares_ref = f32[8,1,128]{2,1,0:T(1,128)S(1)} all-to-all(f32[8,1,128]{2,1,0:T(1,128)S(1)} %get-tuple-element.16), channel_id=1, replica_groups=mesh['row_0'=8,'row_1'=2,'col_0'=4,'col_1'=8] {'col_1'}, dimensions={0} | all-to-all | bytes 8192 | tf_op jit(solution)/shard_map/all_to_all | solution.py:382
  59.5 0.1 shard_map.58
  59.6 24.6 %all_to_all.23 = bf16[64,17,2,128]{3,2,1,0:T(2,128)(2,1)S(1)} all-to-all(bf16[64,17,2,128]{3,2,1,0:T(2,128)(2,1)S(1)} %bitcast.6), channel_id=1, replica_groups=mesh['row_0'=8,'row_1'=2,'col_0'=4,'col_1'=8] {'col_0','row_1','row_0'}, dimensions={0} | all-to-all | bytes 1114112 | tf_op jit(solution)/shard_map/all_to_all | solution.py:389
  84.2 1.4 %shard_map.59 = f32[8,16,1848]{2,1,0:T(8,128)} custom-call(bf16[2176,128]{1,0:T(8,128)(2,1)S(1)} %bitcast.7), custom_call_target="tpu_custom_call" | custom-call | tf_op jit(solution)/shard_map/pallas_call | solution.py:390

commit v8 on v7

--- a/solution.py
+++ b/solution.py
@@ -57,16 +57,9 @@
     ]
     for copy in copies:
         copy.start()
-    for copy in copies:
-        copy.wait()
-    padded[...] = jnp.zeros_like(padded)
-    padded[:, :HALF] = acts_ref[...].astype(F32)
-    plain = padded[...]
-    second_half = lax.rem(lax.axis_index("col_1"), 2) == 1
-    acts = jnp.where(second_half, pltpu.roll(plain, SHIFT, 1), plain)
+    copies[1].wait()
     errs = errs_ref[...].astype(F32)
     low = low_lanes(8)
-    up = 32 * lax.div(lax.axis_index("col_1"), 2)
     lane = lax.broadcasted_iota(jnp.int32, (8, 128), 1)
     quarter = lane[:2] // 32
     err_tiles = []
@@ -79,6 +72,13 @@
             turned = pltpu.roll(both, 32 * v, 1)
             tile = jnp.where(quarter == v, turned[2 * v : 2 * v + 2], tile)
         err_tiles.append(pltpu.roll(tile, 16 * lax.axis_index("row_0"), 1))
+    padded[...] = jnp.zeros_like(padded)
+    copies[0].wait()
+    padded[:, :HALF] = acts_ref[...].astype(F32)
+    plain = padded[...]
+    second_half = lax.rem(lax.axis_index("col_1"), 2) == 1
+    acts = jnp.where(second_half, pltpu.roll(plain, SHIFT, 1), plain)
+    up = 32 * lax.div(lax.axis_index("col_1"), 2)
     for row in range(N_ROW):
         lanes = slice(128 * (row // 2), 128 * (row // 2) + 128)
         upper, lower = acts[:8, lanes], acts[8:, lanes]
@@ -92,6 +92,8 @@
             packed[start : start + 8, :] = tile
             packed[start + 8 : start + 10, :] = err_tiles[z]
     out_ref[...] = packed[: out_ref.shape[0], :].astype(BF16)
+    for copy in copies[2:]:
+        copy.wait()
 
 
 def gather_groups(tiles):

time: 85.9 us -> 86.1 us (level)
  no operation moved by 1% of the time
where the time goes in v8:
time: 86.1 us; the launch traced here: 85.8 us
  blocking collectives  81 us (94%)
  Pallas kernels  4.76 us (6%)
    all_to_all x1, blocking collectives, shards(): packed = lax.all_to_all(packed, Z_ROW, 0, 0, tiled=True)  34 us
    all_to_all x1, blocking collectives, shards(): lax.all_to_all(mixed.reshape(peers, 17, 2, 128), X_ROW, 0, 0, tiled=True)  24.6 us
    all_to_all x1, blocking collectives, shards(): spread = lax.all_to_all(spread, 'col_0', 0, 0, tiled=True)  12.3 us
    all_to_all x1, blocking collectives, shards(): squares = lax.all_to_all(squares, 'col_1', 0, 0, tiled=True)  10.1 us

profile of v8, /device:TPU:1, one launch (start us, length us, event | category | flops | bytes accessed | tf_op | source)
XLA Modules:
  0.0 85.8 jit_solution(12875853530795145419)
XLA Ops:
  0.0 1.3 %shard_map.55 = (bf16[1280,128]{1,0:T(8,128)(2,1)S(1)}, s32[1,32]{1,0:T(1,128)S(1)}, s32[1,16]{1,0:T(1,128)S(1)}, s32[16,32]{1,0:T(8,128)S(1)}) custom-call(bf16[16,924]{1,0:T(8,128)(2,1)} %acts_in.1, bf16[8,256]{1,0:T(8,128)(2,1)} %errs_in.1, s32[1,32]{1,0:T(1,128)} %bitcast.10, s32[1,16]{1,0:T(1,128)} %bitcast.11, s32[16,32]{1,0:T(8,128)} %mask_in.1), custom_call_target="tpu_custom_call" | custom-call | tf_op jit(solution)/shard_map/pallas_call | solution.py:356
  1.3 34.0 %all_to_all.20 = bf16[128,5,2,128]{3,2,1,0:T(2,128)(2,1)S(1)} all-to-all(bf16[128,5,2,128]{3,2,1,0:T(2,128)(2,1)S(1)} %bitcast.9), channel_id=1, replica_groups=mesh['row_0'=8,'row_1'=2,'col_0'=4,'col_1'=8] {'col_1','row_1','row_0'}, dimensions={0} | all-to-all | bytes 655360 | tf_op jit(solution)/shard_map/all_to_all | solution.py:369
  35.3 0.2 shard_map.56
  35.5 12.3 %all_to_all.21.in_ref = bf16[4,512,128]{2,1,0:T(8,128)(2,1)S(1)} all-to-all(bf16[4,512,128]{2,1,0:T(8,128)(2,1)S(1)} %shard_map.56), channel_id=1, replica_groups=mesh['row_0'=8,'row_1'=2,'col_0'=4,'col_1'=8] {'col_0'}, dimensions={0} | all-to-all | bytes 1048576 | tf_op jit(solution)/shard_map/all_to_all | solution.py:376
  47.8 1.7 %shard_map.57 = (bf16[64,32,128]{2,1,0:T(8,128)(2,1)S(1)}, f32[8,1,128]{2,1,0:T(1,128)S(1)}) custom-call(bf16[4,512,128]{2,1,0:T(8,128)(2,1)S(1)} %all_to_all.21.in_ref, s32[1,32]{1,0:T(1,128)S(1)} %get-tuple-element.12.cols_ref, s32[1,16]{1,0:T(1,128)S(1)} %get-tuple-element.13.rows_ref, s32[16,32]{1,0:T(8,128)S(1)} %get-tuple-element.14.mask_ref), custom_call_target="tpu_custom_call" | custom-call | tf_op jit(solution)/shard_map/pallas_call | solution.py:378
  49.5 10.1 %all_to_all.22.squares_ref = f32[8,1,128]{2,1,0:T(1,128)S(1)} all-to-all(f32[8,1,128]{2,1,0:T(1,128)S(1)} %get-tuple-element.16), channel_id=1, replica_groups=mesh['row_0'=8,'row_1'=2,'col_0'=4,'col_1'=8] {'col_1'}, dimensions={0} | all-to-all | bytes 8192 | tf_op jit(solution)/shard_map/all_to_all | solution.py:384
  59.7 0.1 shard_map.58
  59.8 24.6 %all_to_all.23 = bf16[64,17,2,128]{3,2,1,0:T(2,128)(2,1)S(1)} all-to-all(bf16[64,17,2,128]{3,2,1,0:T(2,128)(2,1)S(1)} %bitcast.6), channel_id=1, replica_groups=mesh['row_0'=8,'row_1'=2,'col_0'=4,'col_1'=8] {'col_0','row_1','row_0'}, dimensions={0} | all-to-all | bytes 1114112 | tf_op jit(solution)/shard_map/all_to_all | solution.py:391
  84.4 1.4 %shard_map.59 = f32[8,16,1848]{2,1,0:T(8,128)} custom-call(bf16[2176,128]{1,0:T(8,128)(2,1)S(1)} %bitcast.7), custom_call_target="tpu_custom_call" | custom-call | tf_op jit(solution)/shard_map/pallas_call | solution.py:392
